TPU v7x, 1024 devices: a whole 4x4x32 slice. The times are simulated.
1024 devices in a mesh: lon: 64 (over y, x, z_hi), lat: 16 (over z_lo, core).
Axes of the slice: x: 4, y: 4, z: 32 (z_hi: 4, z_lo: 8; z = z_hi * 8 + z_lo), core: 2. Of those that a mesh axis runs over, the one named last changes fastest.
Arguments:
- thermal_tracer: float32 [6, 512, 8192], P(None, 'lat', 'lon'), may hold values from -6 to 6
- saltiness_tracer: float32 [6, 512, 8192], P(None, 'lat', 'lon'), may hold values from -6 to 6
- eastward_transport: float32 [6, 512, 8192], P(None, 'lat', 'lon'), may hold values from -3 to 3
- northward_transport: float32 [6, 512, 8192], P(None, 'lat', 'lon'), may hold values from -3 to 3
- eastward_spacing: float32 [512, 8192], P('lat', 'lon'), may hold values from 0.25 to 1.75
- southward_spacing: float32 [512, 8192], P('lat', 'lon'), may hold values from 0.25 to 1.75
- ocean_layer_depth: int32 [512, 8192], P('lat', 'lon'), may hold values from 0 to 6
Outputs:
- new_temperature: float32 [6, 512, 8192], P(None, 'lat', 'lon')
- new_salinity: float32 [6, 512, 8192], P(None, 'lat', 'lon')
Inputs may be any that keep to these rules, and one draw needn't show every extreme that they name: ocean_layer_depth[j, i] counts the wet levels of column (j, i); 0 marks land.
All inputs are finite; a program needn't handle non-finite values.
Results may differ from a plain program's by a relative error of at most 0.0003.
Values sent between devices are 32-bit elements; how exact they have to be, the bound alone decides.
A program may use at most 32 MiB of HBM per device.

v0:
```python
import jax
import jax.numpy as jnp
from jax import lax
from jax.sharding import PartitionSpec as P

TIME_STEP = 0.2
DIFFUSIVITY = 0.5
EXPANSION = 0.2
CONTRACTION = 0.8
STRAT_FLOOR = 0.5
SLOPE_LIMIT = 2.0


def partner_2(array, axis, apart):
    return lax.ppermute(array, axis, [(i, i ^ 1 << apart) for i in range(lax.axis_size(axis))])


def padded_2(array, sides, width, wrap):
    for axis, dim in sides:
        count, length = (lax.axis_size(axis), array.shape[dim])
        up = [(i, (i + 1) % count) for i in range(count if wrap else count - 1)]
        down = [(j, i) for i, j in up]
        last = lax.slice_in_dim(array, length - width, length, axis=dim)
        initial = lax.slice_in_dim(array, 0, width, axis=dim)
        before = lax.ppermute(last, axis, up)
        after = lax.ppermute(initial, axis, down)
        array = jnp.concatenate([before, array, after], axis=dim)
    return array


def minmod(first_jump, second_jump):
    return (
        0.5
        * (jnp.sign(first_jump) + jnp.sign(second_jump))
        * jnp.minimum(jnp.abs(first_jump), jnp.abs(second_jump))
    )


def vertical(tracer):
    upper = jnp.concatenate([tracer[:1], tracer[:-1]], 0)
    lower = jnp.concatenate([tracer[1:], tracer[-1:]], 0)
    return 0.5 * (lower - upper)


def face_flux(tracer, density, tracer_dz, density_dz, speed_all, along_all, across_all, wet):
    inner = tracer.shape[-1] - 4
    face_wet = wet[..., :-1] * wet[..., 1:]
    jumps = (tracer[..., 1:] - tracer[..., :-1]) * face_wet
    density_jumps = (density[..., 1:] - density[..., :-1]) * face_wet
    middle = slice(1, inner + 2)
    length = 0.5 * (along_all[..., 1 : inner + 2] + along_all[..., 2 : inner + 3])
    breadth = 0.5 * (across_all[..., 1 : inner + 2] + across_all[..., 2 : inner + 3])
    speed = speed_all[..., middle]
    factor = 0.5 * (1.0 - jnp.abs(speed * TIME_STEP / length))
    left_value = tracer[..., 1 : inner + 2] + factor * minmod(
        jumps[..., 0 : inner + 1], jumps[..., middle]
    )
    right_value = tracer[..., 2 : inner + 3] - factor * minmod(
        jumps[..., middle], jumps[..., 2 : inner + 3]
    )
    upwind = jnp.where(speed >= 0.0, left_value, right_value)
    advective = breadth * speed * face_wet[..., middle] * upwind
    strat = jnp.maximum(
        0.5 * (density_dz[..., 1 : inner + 2] + density_dz[..., 2 : inner + 3]), STRAT_FLOOR
    )
    slope = jnp.clip(density_jumps[..., middle] / length / strat, -SLOPE_LIMIT, SLOPE_LIMIT)
    gradient_z = 0.5 * (tracer_dz[..., 1 : inner + 2] + tracer_dz[..., 2 : inner + 3])
    diffusive = (
        -DIFFUSIVITY
        * breadth
        * face_wet[..., middle]
        * (jumps[..., middle] / length - slope * gradient_z)
    )
    return advective + diffusive


def step_block(padded, layer_pile):
    parallel_sum = padded.shape[1] - 4
    meridian_sum = padded.shape[2] - 4
    width_t = padded[4 * layer_pile]
    height_t = padded[4 * layer_pile + 1]
    bottom = padded[4 * layer_pile + 2]
    level_ids = jnp.arange(layer_pile).astype(padded.dtype)
    wet = (level_ids[:, None, None] < bottom[None]).astype(padded.dtype)
    density = (
        CONTRACTION * padded[layer_pile : 2 * layer_pile] - EXPANSION * padded[0:layer_pile]
    ) * wet
    density_dz = vertical(density)
    rows_in = slice(2, parallel_sum + 2)
    cols_in = slice(2, meridian_sum + 2)

    def turned(source):
        return jnp.swapaxes(source[..., cols_in], -1, -2)

    area = (width_t * height_t)[rows_in, cols_in]
    results = []
    for position in range(2):
        tracer = padded[position * layer_pile : (position + 1) * layer_pile] * wet
        tracer_dz = vertical(tracer)
        flux_x = face_flux(
            tracer[:, rows_in],
            density[:, rows_in],
            tracer_dz[:, rows_in],
            density_dz[:, rows_in],
            padded[2 * layer_pile : 3 * layer_pile, rows_in],
            width_t[None, rows_in],
            height_t[None, rows_in],
            wet[:, rows_in],
        )
        flux_y = jnp.swapaxes(
            face_flux(
                turned(tracer),
                turned(density),
                turned(tracer_dz),
                turned(density_dz),
                turned(padded[3 * layer_pile : 4 * layer_pile]),
                turned(height_t[None]),
                turned(width_t[None]),
                turned(wet),
            ),
            -1,
            -2,
        )
        divergence = flux_x[..., 1:] - flux_x[..., :-1] + (flux_y[:, 1:, :] - flux_y[:, :-1, :])
        updated = tracer[:, rows_in, cols_in] - TIME_STEP * divergence / area
        results.append(wet[:, rows_in, cols_in] * updated)
    return (results[0], results[1])


def local(
    thermal_tracer,
    saltiness_tracer,
    eastward_transport,
    northward_transport,
    eastward_spacing,
    southward_spacing,
    ocean_layer_depth,
):
    layer_pile = thermal_tracer.shape[0]
    parallel_sum = thermal_tracer.shape[1]
    meridian_sum = thermal_tracer.shape[2]
    joined_tracers = jnp.concatenate(
        [
            thermal_tracer,
            saltiness_tracer,
            eastward_transport,
            northward_transport,
            eastward_spacing[None],
            southward_spacing[None],
            ocean_layer_depth.astype(jnp.float32)[None],
        ],
        0,
    )
    factors = jnp.concatenate(
        [
            jnp.ones((2 * layer_pile,), jnp.float32),
            -jnp.ones((2 * layer_pile,), jnp.float32),
            jnp.ones((3,), jnp.float32),
        ]
    )[:, None, None]
    northern = jnp.flip(joined_tracers[:, parallel_sum - 2 :], 1)
    lon_count = lax.axis_size("lon")
    bit_total = lon_count.bit_length() - 1
    bit_order = list(range(bit_total))
    partner = northern
    for bit_number in bit_order:
        partner = partner_2(partner, "lon", bit_number)
    folded = jnp.pad(jnp.flip(partner, -1) * factors, ((0, 0), (0, 0), (2, 2)))
    lat_place = lax.axis_index("lat")
    across = padded_2(joined_tracers, (("lon", 2),), 2, True)
    along = padded_2(joined_tracers, (("lat", 1),), 2, False)
    padded = jnp.zeros((joined_tracers.shape[0], parallel_sum + 4, meridian_sum + 4), jnp.float32)
    padded = padded.at[:, 2 : parallel_sum + 2, :].set(across)
    padded = padded.at[:, :, 2 : meridian_sum + 2].set(along)
    on_top = lat_place == lax.axis_size("lat") - 1
    north_rows = jnp.where(on_top, folded, padded[:, parallel_sum + 2 :])
    padded = padded.at[:, parallel_sum + 2 :].set(north_rows)
    return step_block(padded, layer_pile)


def solution(mesh):
    in_specs = (
        P(None, "lat", "lon"),
        P(None, "lat", "lon"),
        P(None, "lat", "lon"),
        P(None, "lat", "lon"),
        P("lat", "lon"),
        P("lat", "lon"),
        P("lat", "lon"),
    )
    out_specs = (P(None, "lat", "lon"), P(None, "lat", "lon"))
    return jax.shard_map(local, mesh=mesh, in_specs=in_specs, out_specs=out_specs, check_vma=False)
```

profile of v0, /device:TPU:1, one launch (start us, length us, event | category | flops | bytes accessed | tf_op | source)
XLA Modules:
  0.0 178.8 jit_solution(1650120137673714643)
XLA Ops:
  0.6 0.9 constant_dynamic-update-slice_fusion.6
  1.5 0.9 constant_dynamic-update-slice_fusion.5
  2.4 0.9 constant_dynamic-update-slice_fusion.4
  3.3 0.9 constant_dynamic-update-slice_fusion.3
  4.2 0.7 constant_dynamic-update-slice_fusion.2
  4.9 0.7 constant_dynamic-update-slice_fusion.1
  5.7 0.7 constant_dynamic-update-slice_fusion
  6.5 16.3 %collective-permute-start.4 = (f32[27,2,128]{2,1,0:T(2,128)S(1)}, f32[27,2,128]{2,1,0:T(2,128)S(1)}, u32[]{:S(2)}, u32[]{:S(2)}) collective-permute-start(f32[27,2,128]{2,1,0:T(2,128)S(1)} %rev.8), channel_id=1, source_target_pairs={{0,16},{16,0},{32,48},{48,32},{64,80},{80,64},{96,112},{112,96},{1... | collective-permute-start | bytes 82952 | tf_op jit(solution)/shard_map/ppermute | solution.py:15
  22.8 1.2 collective-permute-done.4
  24.0 25.3 %collective-permute-start.5 = (f32[27,2,128]{2,1,0:T(2,128)S(1)}, f32[27,2,128]{2,1,0:T(2,128)S(1)}, u32[]{:S(2)}, u32[]{:S(2)}) collective-permute-start(f32[27,2,128]{2,1,0:T(2,128)S(1)} %collective-permute-done.4), channel_id=1, source_target_pairs={{0,32},{16,48},{32,0},{48,16},{64,96},{80,112},{96,64},{112,80},{1... | collective-permute-start | bytes 82952 | tf_op jit(solution)/shard_map/ppermute | solution.py:15
  49.3 7.7 %collective-permute-start.2 = (f32[27,2,128]{2,1,0:T(2,128)S(1)}, f32[27,2,128]{2,1,0:T(2,128)S(1)}, u32[]{:S(2)}, u32[]{:S(2)}) collective-permute-start(f32[27,2,128]{2,1,0:T(2,128)S(1)} %get-tuple-element.58), channel_id=1, source_target_pairs={{0,1},{1,2},{2,3},{3,4},{4,5},{5,6},{6,7},{7,8},{8,9},{9,10},{10,1... | collective-permute-start | bytes 82952 | tf_op jit(solution)/shard_map/ppermute | solution.py:25
  57.0 1.9 %collective-permute-start.3 = (f32[27,2,128]{2,1,0:T(2,128)S(1)}, f32[27,2,128]{2,1,0:T(2,128)S(1)}, u32[]{:S(2)}, u32[]{:S(2)}) collective-permute-start(f32[27,2,128]{2,1,0:T(2,128)S(1)} %get-tuple-element.59), channel_id=1, source_target_pairs={{1,0},{2,1},{3,2},{4,3},{5,4},{6,5},{7,6},{8,7},{9,8},{10,9},{11,1... | collective-permute-start | bytes 82952 | tf_op jit(solution)/shard_map/ppermute | solution.py:26
  58.9 3.1 %collective-permute-start.6 = (f32[27,2,128]{2,1,0:T(2,128)S(1)}, f32[27,2,128]{2,1,0:T(2,128)S(1)}, u32[]{:S(2)}, u32[]{:S(2)}) collective-permute-start(f32[27,2,128]{2,1,0:T(2,128)S(1)} %collective-permute-done.5), channel_id=1, source_target_pairs={{0,64},{16,80},{32,96},{48,112},{64,0},{80,16},{96,32},{112,48},{1... | collective-permute-start | bytes 82952 | tf_op jit(solution)/shard_map/ppermute | solution.py:15
  62.3 2.8 %collective-permute-start = (f32[27,32,2]{2,1,0:T(8,128)S(1)}, f32[27,32,2]{2,1,0:T(8,128)S(1)}, u32[]{:S(2)}, u32[]{:S(2)}) collective-permute-start(f32[27,32,2]{2,1,0:T(8,128)S(1)} %get-tuple-element.60), channel_id=1, source_target_pairs={{0,16},{16,32},{32,48},{48,64},{64,80},{80,96},{96,112},{112,128},... | collective-permute-start | bytes 20744 | tf_op jit(solution)/shard_map/ppermute | solution.py:25
  65.1 15.4 %collective-permute-start.1 = (f32[27,32,2]{2,1,0:T(8,128)S(1)}, f32[27,32,2]{2,1,0:T(8,128)S(1)}, u32[]{:S(2)}, u32[]{:S(2)}) collective-permute-start(f32[27,32,2]{2,1,0:T(8,128)S(1)} %get-tuple-element.61), channel_id=1, source_target_pairs={{16,0},{32,16},{48,32},{64,48},{80,64},{96,80},{112,96},{128,112},... | collective-permute-start | bytes 20744 | tf_op jit(solution)/shard_map/ppermute | solution.py:26
  80.5 1.9 %collective-permute-start.7 = (f32[27,2,128]{2,1,0:T(2,128)S(1)}, f32[27,2,128]{2,1,0:T(2,128)S(1)}, u32[]{:S(2)}, u32[]{:S(2)}) collective-permute-start(f32[27,2,128]{2,1,0:T(2,128)S(1)} %collective-permute-done.6), channel_id=1, source_target_pairs={{0,128},{16,144},{32,160},{48,176},{64,192},{80,208},{96,224},{112... | collective-permute-start | bytes 82952 | tf_op jit(solution)/shard_map/ppermute | solution.py:15
  82.5 4.5 %collective-permute-done.7 = f32[27,2,128]{2,1,0:T(2,128)S(1)} collective-permute-done((f32[27,2,128]{2,1,0:T(2,128)S(1)}, f32[27,2,128]{2,1,0:T(2,128)S(1)}, u32[]{:S(2)}, u32[]{:S(2)}) %collective-permute-start.7) | collective-permute-done | bytes 27680 | tf_op jit(solution)/shard_map/ppermute | solution.py:15
  86.9 2.7 %collective-permute-start.8 = (f32[27,2,128]{2,1,0:T(2,128)S(1)}, f32[27,2,128]{2,1,0:T(2,128)S(1)}, u32[]{:S(2)}, u32[]{:S(2)}) collective-permute-start(f32[27,2,128]{2,1,0:T(2,128)S(1)} %collective-permute-done.7), channel_id=1, source_target_pairs={{0,256},{16,272},{32,288},{48,304},{64,320},{80,336},{96,352},{112... | collective-permute-start | bytes 82952 | tf_op jit(solution)/shard_map/ppermute | solution.py:15
  89.6 36.8 %collective-permute-done = f32[27,32,2]{2,1,0:T(8,128)S(1)} collective-permute-done((f32[27,32,2]{2,1,0:T(8,128)S(1)}, f32[27,32,2]{2,1,0:T(8,128)S(1)}, u32[]{:S(2)}, u32[]{:S(2)}) %collective-permute-start) | collective-permute-done | bytes 6944 | tf_op jit(solution)/shard_map/ppermute | solution.py:25
  126.5 29.7 %collective-permute-done.1 = f32[27,32,2]{2,1,0:T(8,128)S(1)} collective-permute-done((f32[27,32,2]{2,1,0:T(8,128)S(1)}, f32[27,32,2]{2,1,0:T(8,128)S(1)}, u32[]{:S(2)}, u32[]{:S(2)}) %collective-permute-start.1) | collective-permute-done | bytes 6944 | tf_op jit(solution)/shard_map/ppermute | solution.py:26
  156.7 4.0 %collective-permute-start.9 = (f32[27,2,128]{2,1,0:T(2,128)S(1)}, f32[27,2,128]{2,1,0:T(2,128)S(1)}, u32[]{:S(2)}, u32[]{:S(2)}) collective-permute-start(f32[27,2,128]{2,1,0:T(2,128)S(1)} %collective-permute-done.8), channel_id=1, source_target_pairs={{0,512},{16,528},{32,544},{48,560},{64,576},{80,592},{96,608},{112... | collective-permute-start | bytes 82952 | tf_op jit(solution)/shard_map/ppermute | solution.py:15
  160.8 12.8 %scatter.11 = f32[27,36,132]{2,1,0:T(8,128)S(1)} dynamic-update-slice(f32[27,36,132]{2,1,0:T(8,128)S(1)} %select_maximum_fusion, f32[27,36,128]{2,1,0:T(8,128)S(1)} %pad_maximum_fusion, s32[]{:T(128)} %constant.112.clone.1, s32[]{:T(128)} %constant.112.clone.1, s32[]{:T(128)} %constant.113.clone.1) | dynamic-update-slice | bytes 995332 | tf_op jit(solution)/shard_map/scatter | solution.py:174
  176.0 0.7 fusion.8
  177.9 0.9 fusion.54
  (45 shorter events, 4.3 us)
Async XLA Ops:
  6.5 17.5 %collective-permute-start.4 = (f32[27,2,128]{2,1,0:T(2,128)S(1)}, f32[27,2,128]{2,1,0:T(2,128)S(1)}, u32[]{:S(2)}, u32[]{:S(2)}) collective-permute-start(f32[27,2,128]{2,1,0:T(2,128)S(1)} %rev.8), channel_id=1, source_target_pairs={{0,16},{16,0},{32,48},{48,32},{64,80},{80,64},{96,112},{112,96},{1... | collective-permute-start | bytes 82952 | tf_op jit(solution)/shard_map/ppermute | solution.py:15
  24.0 34.9 %collective-permute-start.5 = (f32[27,2,128]{2,1,0:T(2,128)S(1)}, f32[27,2,128]{2,1,0:T(2,128)S(1)}, u32[]{:S(2)}, u32[]{:S(2)}) collective-permute-start(f32[27,2,128]{2,1,0:T(2,128)S(1)} %collective-permute-done.4), channel_id=1, source_target_pairs={{0,32},{16,48},{32,0},{48,16},{64,96},{80,112},{96,64},{112,80},{1... | collective-permute-start | bytes 82952 | tf_op jit(solution)/shard_map/ppermute | solution.py:15
  49.3 111.4 %collective-permute-start.2 = (f32[27,2,128]{2,1,0:T(2,128)S(1)}, f32[27,2,128]{2,1,0:T(2,128)S(1)}, u32[]{:S(2)}, u32[]{:S(2)}) collective-permute-start(f32[27,2,128]{2,1,0:T(2,128)S(1)} %get-tuple-element.58), channel_id=1, source_target_pairs={{0,1},{1,2},{2,3},{3,4},{4,5},{5,6},{6,7},{7,8},{8,9},{9,10},{10,1... | collective-permute-start | bytes 82952 | tf_op jit(solution)/shard_map/ppermute | solution.py:25
  57.0 103.7 %collective-permute-start.3 = (f32[27,2,128]{2,1,0:T(2,128)S(1)}, f32[27,2,128]{2,1,0:T(2,128)S(1)}, u32[]{:S(2)}, u32[]{:S(2)}) collective-permute-start(f32[27,2,128]{2,1,0:T(2,128)S(1)} %get-tuple-element.59), channel_id=1, source_target_pairs={{1,0},{2,1},{3,2},{4,3},{5,4},{6,5},{7,6},{8,7},{9,8},{10,9},{11,1... | collective-permute-start | bytes 82952 | tf_op jit(solution)/shard_map/ppermute | solution.py:26
  58.9 21.6 %collective-permute-start.6 = (f32[27,2,128]{2,1,0:T(2,128)S(1)}, f32[27,2,128]{2,1,0:T(2,128)S(1)}, u32[]{:S(2)}, u32[]{:S(2)}) collective-permute-start(f32[27,2,128]{2,1,0:T(2,128)S(1)} %collective-permute-done.5), channel_id=1, source_target_pairs={{0,64},{16,80},{32,96},{48,112},{64,0},{80,16},{96,32},{112,48},{1... | collective-permute-start | bytes 82952 | tf_op jit(solution)/shard_map/ppermute | solution.py:15
  62.3 64.2 %collective-permute-start = (f32[27,32,2]{2,1,0:T(8,128)S(1)}, f32[27,32,2]{2,1,0:T(8,128)S(1)}, u32[]{:S(2)}, u32[]{:S(2)}) collective-permute-start(f32[27,32,2]{2,1,0:T(8,128)S(1)} %get-tuple-element.60), channel_id=1, source_target_pairs={{0,16},{16,32},{32,48},{48,64},{64,80},{80,96},{96,112},{112,128},... | collective-permute-start | bytes 20744 | tf_op jit(solution)/shard_map/ppermute | solution.py:25
  65.1 91.1 %collective-permute-start.1 = (f32[27,32,2]{2,1,0:T(8,128)S(1)}, f32[27,32,2]{2,1,0:T(8,128)S(1)}, u32[]{:S(2)}, u32[]{:S(2)}) collective-permute-start(f32[27,32,2]{2,1,0:T(8,128)S(1)} %get-tuple-element.61), channel_id=1, source_target_pairs={{16,0},{32,16},{48,32},{64,48},{80,64},{96,80},{112,96},{128,112},... | collective-permute-start | bytes 20744 | tf_op jit(solution)/shard_map/ppermute | solution.py:26
  80.5 6.4 %collective-permute-start.7 = (f32[27,2,128]{2,1,0:T(2,128)S(1)}, f32[27,2,128]{2,1,0:T(2,128)S(1)}, u32[]{:S(2)}, u32[]{:S(2)}) collective-permute-start(f32[27,2,128]{2,1,0:T(2,128)S(1)} %collective-permute-done.6), channel_id=1, source_target_pairs={{0,128},{16,144},{32,160},{48,176},{64,192},{80,208},{96,224},{112... | collective-permute-start | bytes 82952 | tf_op jit(solution)/shard_map/ppermute | solution.py:15
  86.9 69.8 %collective-permute-start.8 = (f32[27,2,128]{2,1,0:T(2,128)S(1)}, f32[27,2,128]{2,1,0:T(2,128)S(1)}, u32[]{:S(2)}, u32[]{:S(2)}) collective-permute-start(f32[27,2,128]{2,1,0:T(2,128)S(1)} %collective-permute-done.7), channel_id=1, source_target_pairs={{0,256},{16,272},{32,288},{48,304},{64,320},{80,336},{96,352},{112... | collective-permute-start | bytes 82952 | tf_op jit(solution)/shard_map/ppermute | solution.py:15
  156.7 17.1 %copy-start = (f32[27]{0:T(128)S(1)}, f32[27]{0:T(128)}, u32[]{:S(2)}) copy-start(f32[27]{0:T(128)} %constant.116.clone.1) | copy-start | bytes 328
  156.7 16.9 %collective-permute-start.9 = (f32[27,2,128]{2,1,0:T(2,128)S(1)}, f32[27,2,128]{2,1,0:T(2,128)S(1)}, u32[]{:S(2)}, u32[]{:S(2)}) collective-permute-start(f32[27,2,128]{2,1,0:T(2,128)S(1)} %collective-permute-done.8), channel_id=1, source_target_pairs={{0,512},{16,528},{32,544},{48,560},{64,576},{80,592},{96,608},{112... | collective-permute-start | bytes 82952 | tf_op jit(solution)/shard_map/ppermute | solution.py:15
where the time goes:
time: 179 us
  starting transfers between devices  81.2 us (45%)
  waiting for transfers between devices  72.3 us (40%)
  local copies, waits for them, and re-layouts  19.1 us (11%)
  other arithmetic  5.25 us (3%)
    ppermute x6, starting transfers between devices, partner_2(): lax.ppermute(array, axis, [(i, i ^ 1 << apart) for i in range(lax.axis_si...  53.3 us
    ppermute x2, waiting for transfers between devices, padded_2(): before = lax.ppermute(last, axis, up)  36.8 us
    ppermute x2, waiting for transfers between devices, padded_2(): after = lax.ppermute(initial, axis, down)  29.7 us
    ppermute x2, starting transfers between devices, padded_2(): after = lax.ppermute(initial, axis, down)  17.4 us
    scatter x1, local copies, waits for them, and re-layouts, local(): padded = padded.at[:, :, 2:meridian_sum + 2].set(along)  12.8 us
    ppermute x2, starting transfers between devices, padded_2(): before = lax.ppermute(last, axis, up)  10.5 us
    ppermute x6, waiting for transfers between devices, partner_2(): lax.ppermute(array, axis, [(i, i ^ 1 << apart) for i in range(lax.axis_si...  5.7 us
    unnamed x8, local copies, waits for them, and re-layouts  5.04 us
  transfers between devices with their start and end apart: 10, of which 4 were waited for; matrix products, arithmetic and copies ran while one was open for 8% of the time, Pallas kernels for 0%

commit v1 on v0

v1 whole, which is shorter than its diff:
```python
import jax
import jax.numpy as jnp
from jax import lax
from jax.experimental import pallas as pl
from jax.experimental.pallas import tpu as pltpu
from jax.sharding import PartitionSpec as P

MESH = pl.DeviceIdType.MESH
F32 = jnp.float32

TIME_STEP = 0.2
DIFFUSIVITY = 0.5
EXPANSION = 0.2
CONTRACTION = 0.8
STRAT_FLOOR = 0.5
SLOPE_LIMIT = 2.0

LEVELS = 6
ROWS = 32
LANES = 128


def turn(x, shift, axis):
    shift = shift % x.shape[axis]
    return x if shift == 0 else pltpu.roll(x, shift, axis)


def lane_reversed(x, lane):
    for bit in range(7):
        step = 1 << bit
        x = jnp.where((lane & step) == 0, turn(x, -step, 1), turn(x, step, 1))
    return x


def face_terms(speed, rlen):
    return speed >= 0.0, 0.5 - jnp.abs((0.5 * TIME_STEP) * speed * rlen)


def face_slope(rjump, rlen, strat):
    return jnp.clip(rjump * rlen / jnp.maximum(strat, STRAT_FLOOR), -SLOPE_LIMIT, SLOPE_LIMIT)


def face_flux(here, there, before, jump, after, gradient, slope, speed, upwind, factor, rlen):
    side = jnp.where(upwind, before, after)
    limited = jnp.maximum(jnp.minimum(side, jump), 0.0) + jnp.minimum(jnp.maximum(side, jump), 0.0)
    step = factor * limited
    value = jnp.where(upwind, here + step, there - step)
    return speed * value - DIFFUSIVITY * (jump * rlen - slope * gradient)


def vertical_quarter(sums):
    count = len(sums)
    return [0.25 * (sums[min(k + 1, count - 1)] - sums[max(k - 1, 0)]) for k in range(count)]


def kernel(
    temp_hbm, salt_hbm, east_hbm, north_hbm, dx_hbm, dy_hbm, depth_hbm,
    new_temp, new_salt,
    temp_in, salt_in, east_in, north_in, dx_in, dy_in, depth_in,
    held, result,
    pack_ts, pack_u, pack_g,
    own_rows, own_speed, own_geo,
    to_east, to_west, to_north, to_south,
    from_west, from_east, from_south, from_north,
    in_sem, out_sem, send_sem, recv_sem,
):
    lon, lat = lax.axis_index("lon"), lax.axis_index("lat")
    lon_count, lat_count = lax.axis_size("lon"), lax.axis_size("lat")
    west = (lax.rem(lon + lon_count - 1, lon_count), lat)
    east = (lax.rem(lon + 1, lon_count), lat)
    mirror = (lon_count - 1 - lon, lat)
    top = lat == lat_count - 1
    bottom = lat == 0

    barrier = pltpu.get_barrier_semaphore()

    def greet(device):
        pl.semaphore_signal(barrier, inc=1, device_id=device, device_id_type=MESH)

    greet(west)
    greet(east)

    @pl.when(top)
    def _():
        greet(mirror)

    @pl.when(jnp.logical_not(top))
    def _():
        greet((lon, lat + 1))

    @pl.when(jnp.logical_not(bottom))
    def _():
        greet((lon, lat - 1))

    pairs = [
        (depth_hbm, depth_in), (temp_hbm, temp_in), (salt_hbm, salt_in), (east_hbm, east_in),
        (dx_hbm, dx_in), (dy_hbm, dy_in), (north_hbm, north_in),
    ]
    loads = [pltpu.make_async_copy(a, b, in_sem.at[i]) for i, (a, b) in enumerate(pairs)]
    for load in loads:
        load.start()
    for load in loads:
        load.wait()

    lane8 = lax.broadcasted_iota(jnp.int32, (8, LANES), 1)
    sub8 = lax.broadcasted_iota(jnp.int32, (8, LANES), 0)
    slot = lane8 & 15
    group = lane8 >> 4

    depth = depth_in[...].astype(F32)
    for k in range(LEVELS):
        wet = depth > float(k)
        held[0, k] = jnp.where(wet, temp_in[k], 0.0)
        held[1, k] = jnp.where(wet, salt_in[k], 0.0)

    def gathered(blocks):
        total = turn(blocks[0], 4, 1)
        for g in range(1, len(blocks)):
            total = jnp.where(group == g, turn(blocks[g], 16 * g + 4, 1), total)
        return total

    def blocks_of(array):
        return [array[8 * r : 8 * r + 8] for r in range(ROWS // 8)]

    packed = []
    packed_u = []
    for k in range(LEVELS):
        packed.append(gathered(blocks_of(held[0, k]) + blocks_of(held[1, k])))
        packed_u.append(gathered(blocks_of(east_in[k]) * 2))
    dx, dy = dx_in[...], dy_in[...]
    packed_d = gathered(blocks_of(depth) * 2)
    packed_dx = gathered(blocks_of(dx) * 2)
    packed_dy = gathered(blocks_of(dy) * 2)

    eastward, westward, eastward_u = packed_d, packed_d, packed_d
    eastward, westward = turn(packed_d, 10, 1), turn(packed_d, 8, 1)
    eastward = jnp.where(slot == 14, turn(packed_dx, 11, 1), eastward)
    eastward = jnp.where(slot == 15, turn(packed_dy, 12, 1), eastward)
    westward = jnp.where(slot == 14, turn(packed_dx, 10, 1), westward)
    westward = jnp.where(slot == 15, turn(packed_dy, 11, 1), westward)
    eastward_u = turn(packed_u[0], -3, 1)
    for k in range(LEVELS):
        eastward = jnp.where((slot >> 1) == k, turn(packed[k], 2 * k - 2, 1), eastward)
        westward = jnp.where((slot >> 1) == k, turn(packed[k], 2 * k - 4, 1), westward)
        if k:
            eastward_u = jnp.where(slot == k, turn(packed_u[k], k - 3, 1), eastward_u)
    to_east[0:8] = eastward
    to_east[8:16] = eastward_u
    to_west[...] = westward

    for k in range(LEVELS):
        at = 8 * (k // 2) + 2 * (k % 2)
        for tracer in range(2):
            to_north[at + 4 * tracer : at + 4 * tracer + 2] = held[tracer, k, ROWS - 2 : ROWS]
            to_south[at + 4 * tracer : at + 4 * tracer + 2] = held[tracer, k, 0:2]
        to_north[28 + k : 29 + k] = north_in[k, ROWS - 1 : ROWS]
    to_north[24:26] = depth[ROWS - 2 : ROWS]
    to_north[26:27] = dx_in[ROWS - 1 : ROWS]
    to_north[27:28] = dy_in[ROWS - 1 : ROWS]
    to_north[34:40] = jnp.zeros((6, LANES), F32)
    to_south[24:26] = depth[0:2]
    to_south[26:27] = dx_in[0:1]
    to_south[27:28] = dy_in[0:1]
    to_south[28:32] = jnp.zeros((4, LANES), F32)

    @pl.when(top)
    def _():
        for block in range(4):
            x = to_north[8 * block : 8 * block + 8]
            swapped = jnp.where((sub8 & 1) == 0, turn(x, -1, 0), turn(x, 1, 0))
            if block == 3:
                swapped = jnp.where(sub8 < 2, swapped, x)
            to_north[8 * block : 8 * block + 8] = lane_reversed(swapped, lane8)

    @pl.when(bottom)
    def _():
        from_south[...] = jnp.zeros_like(from_south)

    pl.semaphore_wait(barrier, jnp.where(bottom, 3, 4))

    def remote(src, dst, index, device):
        return pltpu.make_async_remote_copy(
            src_ref=src, dst_ref=dst, send_sem=send_sem.at[index], recv_sem=recv_sem.at[index],
            device_id=device, device_id_type=MESH,
        )

    send_east = remote(to_east, from_west, 0, east)
    send_west = remote(to_west, from_east, 1, west)

    send_north = remote(to_north, from_south, 2, (lon, jnp.minimum(lat + 1, lat_count - 1)))
    send_south = remote(to_south, from_north, 3, (lon, jnp.maximum(lat - 1, 0)))
    send_east.start()
    send_west.start()

    @pl.when(top)
    def _():
        pltpu.make_async_remote_copy(
            src_ref=to_north.at[0:32], dst_ref=from_north, send_sem=send_sem.at[2], recv_sem=recv_sem.at[3],
            device_id=mirror, device_id_type=MESH,
        ).start()

    @pl.when(jnp.logical_not(top))
    def _():
        send_north.start()

    @pl.when(jnp.logical_not(bottom))
    def _():
        send_south.start()

    def opened(x):
        return jnp.where(slot < 4, x, turn(x, 4, 1))

    for k in range(LEVELS):
        pack_ts[k] = opened(packed[k])
        pack_u[k] = opened(packed_u[k])
    pack_g[0] = opened(packed_d)
    pack_g[1] = opened(packed_dx)
    pack_g[2] = opened(packed_dy)

    lane = lax.broadcasted_iota(jnp.int32, (ROWS, LANES), 1)
    row = lax.broadcasted_iota(jnp.int32, (ROWS, LANES), 0)
    inside_x = (lane >= 1) & (lane <= LANES - 3)
    inside_y = (row >= 1) & (row <= ROWS - 3)
    scale = -TIME_STEP / (dx * dy)

    def axis_part(axis, along, across, inside):
        size = LANES if axis else ROWS
        rlen = 2.0 / (along + turn(along, -1, axis))
        breadth = jnp.where(inside, 0.5 * (across + turn(across, -1, axis)), 0.0)
        least = jnp.minimum(depth, turn(depth, -1, axis))
        return rlen, breadth, least

    geo = [axis_part(1, dx, dy, inside_x), axis_part(0, dy, dx, inside_y)]

    def level_state(k):
        t, s = held[0, k], held[1, k]
        return [(t, s, turn(t, -1, a), turn(s, -1, a)) for a in (1, 0)]

    states = [level_state(k) for k in range(LEVELS)]
    for k in range(LEVELS):
        divergence = [0.0, 0.0]
        for position, axis in enumerate((1, 0)):
            rlen, breadth, least = geo[position]
            t, s, t1, s1 = states[k][position]
            up, down = states[min(k + 1, LEVELS - 1)][position], states[max(k - 1, 0)][position]
            gt = 0.25 * ((up[0] + up[2]) - (down[0] + down[2]))
            gs = 0.25 * ((up[1] + up[3]) - (down[1] + down[3]))
            face = least > float(k)
            jt = jnp.where(face, t1 - t, 0.0)
            js = jnp.where(face, s1 - s, 0.0)
            speed = (east_in if axis else north_in)[k]
            upwind, factor = face_terms(speed, rlen)
            slope = face_slope(CONTRACTION * js - EXPANSION * jt, rlen, CONTRACTION * gs - EXPANSION * gt)
            weight = jnp.where(face, breadth, 0.0)
            for tracer, (a, b, j, g) in enumerate(((t, t1, jt, gt), (s, s1, js, gs))):
                flux = weight * face_flux(
                    a, b, turn(j, 1, axis), j, turn(j, -1, axis), g, slope, speed, upwind, factor, rlen
                )
                divergence[tracer] = divergence[tracer] + (flux - turn(flux, 1, axis))
        wet = depth > float(k)
        for tracer in range(2):
            result[tracer, k] = held[tracer, k] + jnp.where(wet, scale * divergence[tracer], 0.0)

    odd = sub8 & 3
    own_mix = jnp.where(sub8 < 4, -EXPANSION, CONTRACTION)
    other_mix = jnp.where(sub8 < 4, CONTRACTION, -EXPANSION)
    lane_mix = jnp.where(lane8 < 64, -EXPANSION, CONTRACTION)
    lane_other = jnp.where(lane8 < 64, CONTRACTION, -EXPANSION)

    spans = ((2, 4, 29, 31), (1, 2, 0, 1), (2, 4, 30, 32), (0, 2, 0, 2), (2, 3, 31, 32), (0, 2, 1, 3))
    places = (0, 1, 1, 2, 2, 3)
    for place, (lo, hi, first, last) in zip(places, spans):
        for tracer in range(2):
            at = 4 * tracer
            for k in range(LEVELS):
                own_rows[place, k, at + lo : at + hi] = held[tracer, k, first:last]
            own_geo[place, at + lo : at + hi] = depth[first:last]
    for tracer in range(2):
        at = 4 * tracer
        for k in range(LEVELS):
            own_speed[k, at + 1 : at + 2] = north_in[k, 0:1]
            own_speed[k, at + 2 : at + 4] = north_in[k, 30:32]
        for which, source in ((4, dx_in), (6, dy_in)):
            own_geo[which, at + 1 : at + 2] = source[0:1]
            own_geo[which, at + 2 : at + 4] = source[30:32]
            own_geo[which + 1, at : at + 2] = source[0:2]
            own_geo[which + 1, at + 2 : at + 3] = source[31:32]
        own_geo[8, at : at + 2] = scale[0:2]
        own_geo[8, at + 2 : at + 4] = scale[30:32]
        own_geo[9, at : at + 2] = depth[0:2]
        own_geo[9, at + 2 : at + 4] = depth[30:32]

    @pl.when(jnp.logical_not(bottom))
    def _():
        remote(to_north, from_south, 2, (lon, lat)).wait_recv()

    remote(to_south, from_north, 3, (lon, lat)).wait_recv()

    def spread(ref, index):
        return jnp.broadcast_to(ref[index : index + 1], (8, LANES))

    depth_a = jnp.where(odd == 0, spread(from_south, 24), jnp.where(odd == 1, spread(from_south, 25), own_geo[0]))
    depth_b = jnp.where(odd == 0, spread(from_south, 25), own_geo[1])
    depth_c = jnp.where(odd == 3, spread(from_north, 24), own_geo[2])
    depth_d = jnp.where(odd == 2, spread(from_north, 24), jnp.where(odd == 3, spread(from_north, 25), own_geo[3]))
    dx_b = jnp.where(odd == 0, spread(from_south, 26), own_geo[4])
    dx_c = jnp.where(odd == 3, spread(from_north, 26), own_geo[5])
    dy_b = jnp.where(odd == 0, spread(from_south, 27), own_geo[6])
    dy_c = jnp.where(odd == 3, spread(from_north, 27), own_geo[7])
    rlen = 2.0 / (dy_b + dy_c)
    breadth = 0.5 * (dx_b + dx_c)
    least_w, least_m, least_e = (
        jnp.minimum(depth_a, depth_b), jnp.minimum(depth_b, depth_c), jnp.minimum(depth_c, depth_d)
    )
    operands = []
    for k in range(LEVELS):
        south = from_south[8 * (k // 2) : 8 * (k // 2) + 8]
        north = from_north[8 * (k // 2) : 8 * (k // 2) + 8]
        south = turn(south, -2 * (k % 2), 0)
        north = turn(north, 2 - 2 * (k % 2), 0)
        operands.append((
            jnp.where(odd < 2, south, own_rows[0, k]),
            jnp.where(odd == 0, turn(south, -1, 0), own_rows[1, k]),
            jnp.where(odd == 3, turn(north, 1, 0), own_rows[2, k]),
            jnp.where(odd >= 2, north, own_rows[3, k]),
        ))
    gradients = vertical_quarter([b + c for _, b, c, _ in operands])
    for k in range(LEVELS):
        a, b, c, d = operands[k]
        jump = jnp.where(least_m > float(k), c - b, 0.0)
        before = jnp.where(least_w > float(k), b - a, 0.0)
        after = jnp.where(least_e > float(k), d - c, 0.0)
        gradient = gradients[k]
        speed = jnp.where(odd == 0, spread(from_south, 28 + k), own_speed[k])
        upwind, factor = face_terms(speed, rlen)
        slope = face_slope(
            own_mix * jump + other_mix * turn(jump, 4, 0), rlen, own_mix * gradient + other_mix * turn(gradient, 4, 0)
        )
        flux = jnp.where(least_m > float(k), breadth, 0.0) * face_flux(
            b, c, before, jump, after, gradient, slope, speed, upwind, factor, rlen
        )
        change = jnp.where(
            odd == 0, turn(flux, -1, 0) - flux,
            jnp.where(odd == 1, -flux, jnp.where(odd == 2, flux, flux - turn(flux, 1, 0))),
        )
        change = jnp.where(own_geo[9] > float(k), own_geo[8] * change, 0.0)
        for tracer in range(2):
            at = 4 * tracer
            result[tracer, k, 0:2] += change[at : at + 2]
            result[tracer, k, ROWS - 2 : ROWS] += change[at + 2 : at + 4]

    remote(to_east, from_west, 0, (lon, lat)).wait_recv()
    remote(to_west, from_east, 1, (lon, lat)).wait_recv()
    came_w, came_u, came_e = from_west[0:8], from_west[8:16], from_east[...]

    def closed(own, low, high, low_from, high_from):
        x = jnp.where((slot >> 1) == 3, turn(low, 6 - low_from, 1), own)
        return jnp.where((slot >> 1) == 2, turn(high, 4 - high_from, 1), x)

    depth_x = closed(pack_g[0], came_w, came_e, 12, 12)
    own_dx, own_dy = pack_g[1], pack_g[2]
    dx_x = closed(own_dx, came_w, came_e, 13, 14)
    dy_x = closed(own_dy, came_w, came_e, 14, 15)
    rlen = 2.0 / (dx_x + turn(dx_x, -1, 1))
    breadth = 0.5 * (dy_x + turn(dy_x, -1, 1))
    edge = (slot == 2) | (slot == 3) | (slot == 7) | (slot == 8)
    breadth = jnp.where(edge, breadth, 0.0)
    least = jnp.minimum(depth_x, turn(depth_x, -1, 1))
    weight_x = -TIME_STEP / (dx_x * dy_x)
    values = [closed(pack_ts[k], came_w, came_e, 2 * k, 2 * k) for k in range(LEVELS)]
    nexts = [turn(x, -1, 1) for x in values]
    gradients = vertical_quarter([x + y for x, y in zip(values, nexts)])
    for k in range(LEVELS):
        face = least > float(k)
        jump = jnp.where(face, nexts[k] - values[k], 0.0)
        gradient = gradients[k]
        speed = jnp.where(slot == 7, turn(came_u, 7 - k, 1), pack_u[k])
        upwind, factor = face_terms(speed, rlen)
        slope = face_slope(
            lane_mix * jump + lane_other * turn(jump, 64, 1), rlen,
            lane_mix * gradient + lane_other * turn(gradient, 64, 1),
        )
        flux = jnp.where(face, breadth, 0.0) * face_flux(
            values[k], nexts[k], turn(jump, 1, 1), jump, turn(jump, -1, 1), gradient, slope, speed, upwind, factor,
            rlen,
        )
        change = flux - turn(flux, 1, 1)
        change = jnp.where(depth_x > float(k), weight_x * change, 0.0)
        change = jnp.where(slot < 4, change, turn(change, -4, 1))
        for tracer in range(2):
            for r in range(ROWS // 8):
                moved = turn(change, 124 - 64 * tracer - 16 * r, 1)
                result[tracer, k, 8 * r : 8 * r + 8] += jnp.where((lane8 < 2) | (lane8 >= 126), moved, 0.0)

    stores = [
        pltpu.make_async_copy(result.at[0], new_temp, out_sem.at[0]),
        pltpu.make_async_copy(result.at[1], new_salt, out_sem.at[1]),
    ]
    for store in stores:
        store.start()
    send_east.wait_send()
    send_west.wait_send()

    @pl.when(top)
    def _():
        pltpu.make_async_remote_copy(
            src_ref=to_north.at[0:32], dst_ref=from_north, send_sem=send_sem.at[2], recv_sem=recv_sem.at[3],
            device_id=mirror, device_id_type=MESH,
        ).wait_send()

    @pl.when(jnp.logical_not(top))
    def _():
        send_north.wait_send()

    @pl.when(jnp.logical_not(bottom))
    def _():
        send_south.wait_send()

    for store in stores:
        store.wait()


def local(temp, salt, east, north, dx, dy, depth):
    full = (LEVELS, ROWS, LANES)
    flat = (ROWS, LANES)
    shape = jax.ShapeDtypeStruct(full, F32)
    scratch = [
        pltpu.VMEM(full, F32), pltpu.VMEM(full, F32), pltpu.VMEM(full, F32), pltpu.VMEM(full, F32),
        pltpu.VMEM(flat, F32), pltpu.VMEM(flat, F32), pltpu.VMEM(flat, jnp.int32),
        pltpu.VMEM((2,) + full, F32), pltpu.VMEM((2,) + full, F32),
        pltpu.VMEM((LEVELS, 8, LANES), F32), pltpu.VMEM((LEVELS, 8, LANES), F32), pltpu.VMEM((3, 8, LANES), F32),
        pltpu.VMEM((4, LEVELS, 8, LANES), F32), pltpu.VMEM((LEVELS, 8, LANES), F32), pltpu.VMEM((10, 8, LANES), F32),
        pltpu.VMEM((16, LANES), F32), pltpu.VMEM((8, LANES), F32), pltpu.VMEM((40, LANES), F32), pltpu.VMEM((32, LANES), F32),
        pltpu.VMEM((16, LANES), F32), pltpu.VMEM((8, LANES), F32), pltpu.VMEM((40, LANES), F32), pltpu.VMEM((32, LANES), F32),
        pltpu.SemaphoreType.DMA((7,)), pltpu.SemaphoreType.DMA((2,)),
        pltpu.SemaphoreType.DMA((4,)), pltpu.SemaphoreType.DMA((4,)),
    ]
    return pl.pallas_call(
        kernel,
        out_shape=(shape, shape),
        in_specs=[pl.BlockSpec(memory_space=pl.ANY)] * 7,
        out_specs=(pl.BlockSpec(memory_space=pl.ANY),) * 2,
        scratch_shapes=scratch,
        compiler_params=pltpu.CompilerParams(collective_id=0, has_side_effects=True),
        name="tracer_step",
    )(temp, salt, east, north, dx, dy, depth)


def solution(mesh):
    full = P(None, "lat", "lon")
    flat = P("lat", "lon")
    return jax.shard_map(
        local, mesh=mesh, in_specs=(full,) * 4 + (flat,) * 3, out_specs=(full, full), check_vma=False
    )
```

time: 179 us -> 38.7 us (0.22)
  starting transfers between devices: 81.2 us -> 0 us
  waiting for transfers between devices: 72.3 us -> 0 us
  Pallas kernels: 0 us -> 35.7 us
  local copies, waits for them, and re-layouts: 19.1 us -> 2.22 us
  other arithmetic: 5.25 us -> 0 us
    ppermute x10 -> x0, starting transfers between devices: 81.2 us -> none  [the longest x6 53.3 us: partner_2(): lax.ppermute(array, axis, [(i, i ^ 1 << apart) for i in range(lax.axis_si...]
    ppermute x10 -> x0, waiting for transfers between devices: 72.3 us -> none  [the longest x2 36.8 us: padded_2(): before = lax.ppermute(last, axis, up)]
    pallas_call x0 -> x1, Pallas kernels: none -> 35.7 us  [local(): pl.pallas_call(kernel, out_shape=(shape, shape), in_specs=[pl.BlockSpec(m...]
    scatter x1 -> x0, local copies, waits for them, and re-layouts: 12.8 us -> none  [local(): padded = padded.at[:, :, 2:meridian_sum + 2].set(along)]
    unnamed x8 -> x4, local copies, waits for them, and re-layouts: 5.04 us -> 2.22 us
  transfers between devices with their start and end apart: 10 -> 0, of which waited for: 4 -> 0; matrix products, arithmetic and copies ran while one was open for 8% -> 0% of each run, Pallas kernels for 0% -> 0%
where the time goes in v1:
time: 38.7 us; the launch traced here: 38.5 us
  Pallas kernels  35.7 us (92%)
  local copies, waits for them, and re-layouts  2.22 us (6%)
  between operations  0.65 us (2%)
    pallas_call x1, Pallas kernels, local(): pl.pallas_call(kernel, out_shape=(shape, shape), in_specs=[pl.BlockSpec(m...  35.7 us
    unnamed x4, local copies, waits for them, and re-layouts  2.22 us

profile of v1, /device:TPU:1, one launch (start us, length us, event | category | flops | bytes accessed | tf_op | source)
XLA Modules:
  0.0 38.5 jit_solution(1929066833069334209)
XLA Ops:
  0.6 35.7 %tracer_step.1 = (f32[6,32,128]{2,1,0:T(8,128)}, f32[6,32,128]{2,1,0:T(8,128)}) custom-call(f32[6,32,128]{2,1,0:T(8,128)} %temp_hbm.1, f32[6,32,128]{2,1,0:T(8,128)} %salt_hbm.1, f32[6,32,128]{2,1,0:T(8,128)} %east_hbm.1, f32[6,32,128]{2,1,0:T(8,128)} %north_hbm.1, f32[32,128]{1,0:T(8,128)} %dx_hbm.1, f32[32,128]{1,0:T(8,128)} %dy_hbm.1, s32[32,128]{1,0:T(8,128)} %depth_hbm.1), custom_call_target="tpu_custom_call" | custom-call | tf_op jit(solution)/shard_map/tracer_step/pallas_call | solution.py:438
  36.3 0.0 copy-start
  36.3 1.6 %copy.11 = f32[6,32,128]{2,1,0:T(8,128)} copy(f32[6,32,128]{2,1,0:T(8,128)} %get-tuple-element.4) | data formatting | bytes 196608
  37.9 0.0 copy-done
  37.9 0.6 %copy.12 = f32[6,32,128]{2,1,0:T(8,128)} copy(f32[6,32,128]{2,1,0:T(8,128)S(1)} %copy-done) | data formatting | bytes 196608
Async XLA Ops:
  36.3 1.6 %copy-start = (f32[6,32,128]{2,1,0:T(8,128)S(1)}, f32[6,32,128]{2,1,0:T(8,128)}, u32[]{:S(2)}) copy-start(f32[6,32,128]{2,1,0:T(8,128)} %get-tuple-element.5) | copy-start | bytes 294916

commit v2 on v1

--- a/solution.py
+++ b/solution.py
@@ -55,42 +55,35 @@
 
 def kernel(
     temp_hbm, salt_hbm, east_hbm, north_hbm, dx_hbm, dy_hbm, depth_hbm,
-    new_temp, new_salt,
+    result, changes,
     temp_in, salt_in, east_in, north_in, dx_in, dy_in, depth_in,
-    held, result,
+    held,
     pack_ts, pack_u, pack_g,
     own_rows, own_speed, own_geo,
     to_east, to_west, to_north, to_south,
     from_west, from_east, from_south, from_north,
-    in_sem, out_sem, send_sem, recv_sem,
+    in_sem, send_sem, recv_sem,
 ):
     lon, lat = lax.axis_index("lon"), lax.axis_index("lat")
     lon_count, lat_count = lax.axis_size("lon"), lax.axis_size("lat")
     west = (lax.rem(lon + lon_count - 1, lon_count), lat)
     east = (lax.rem(lon + 1, lon_count), lat)
     mirror = (lon_count - 1 - lon, lat)
+    north = (lon, jnp.minimum(lat + 1, lat_count - 1))
+    south = (lon, jnp.maximum(lat - 1, 0))
     top = lat == lat_count - 1
     bottom = lat == 0
 
-    barrier = pltpu.get_barrier_semaphore()
-
-    def greet(device):
-        pl.semaphore_signal(barrier, inc=1, device_id=device, device_id_type=MESH)
-
-    greet(west)
-    greet(east)
-
-    @pl.when(top)
-    def _():
-        greet(mirror)
-
-    @pl.when(jnp.logical_not(top))
-    def _():
-        greet((lon, lat + 1))
-
-    @pl.when(jnp.logical_not(bottom))
-    def _():
-        greet((lon, lat - 1))
+    place = lax.rem(lon, 4)
+    even = lax.rem(lat, 2) == 0
+    leads_east = place >= 2
+    leads_west = (place == 1) | (place == 2)
+    leads_mirror = place >= 2
+    leads_north = even | (top & leads_mirror)
+    leads_south = even & jnp.logical_not(bottom)
+    answers_east = place <= 1
+    answers_west = (place == 0) | (place == 3)
+    answers_south = jnp.logical_not(even)
 
     pairs = [
         (depth_hbm, depth_in), (temp_hbm, temp_in), (salt_hbm, salt_in), (east_hbm, east_in),
@@ -99,7 +92,70 @@
     loads = [pltpu.make_async_copy(a, b, in_sem.at[i]) for i, (a, b) in enumerate(pairs)]
     for load in loads:
         load.start()
-    for load in loads:
+
+    barrier = pltpu.get_barrier_semaphore()
+
+    def greet(device):
+        pl.semaphore_signal(barrier, inc=1, device_id=device, device_id_type=MESH)
+
+    @pl.when(answers_east)
+    def _():
+        greet(east)
+
+    @pl.when(answers_west)
+    def _():
+        greet(west)
+
+    @pl.when(jnp.logical_not(even))
+    def _():
+        greet(south)
+
+    @pl.when(jnp.logical_not(even | top))
+    def _():
+        greet(north)
+
+    @pl.when(top & jnp.logical_not(leads_mirror))
+    def _():
+        greet(mirror)
+
+    def one(flag):
+        return jnp.where(flag, 1, 0)
+
+    announced = (
+        one(leads_east) + one(leads_west) + one(even) + one(leads_south) + one(top & leads_mirror)
+    )
+
+    def remote(src, dst, out, into, device):
+        return pltpu.make_async_remote_copy(
+            src_ref=src, dst_ref=dst, send_sem=send_sem.at[out], recv_sem=recv_sem.at[into],
+            device_id=device, device_id_type=MESH,
+        )
+
+    def send_east():
+        return remote(to_east, from_west, 0, 0, east)
+
+    def send_west():
+        return remote(to_west, from_east, 1, 1, west)
+
+    def send_north():
+        return remote(to_north, from_south, 2, 2, north)
+
+    def send_mirror():
+        return remote(to_north.at[0:32], from_north, 2, 3, mirror)
+
+    def send_south():
+        return remote(to_south, from_north, 3, 3, south)
+
+    def start_northward():
+        @pl.when(top)
+        def _():
+            send_mirror().start()
+
+        @pl.when(jnp.logical_not(top))
+        def _():
+            send_north().start()
+
+    for load in loads[:3]:
         load.wait()
 
     lane8 = lax.broadcasted_iota(jnp.int32, (8, LANES), 1)
@@ -126,13 +182,15 @@
     packed_u = []
     for k in range(LEVELS):
         packed.append(gathered(blocks_of(held[0, k]) + blocks_of(held[1, k])))
+    for load in loads[3:6]:
+        load.wait()
+    for k in range(LEVELS):
         packed_u.append(gathered(blocks_of(east_in[k]) * 2))
     dx, dy = dx_in[...], dy_in[...]
     packed_d = gathered(blocks_of(depth) * 2)
     packed_dx = gathered(blocks_of(dx) * 2)
     packed_dy = gathered(blocks_of(dy) * 2)
 
-    eastward, westward, eastward_u = packed_d, packed_d, packed_d
     eastward, westward = turn(packed_d, 10, 1), turn(packed_d, 8, 1)
     eastward = jnp.where(slot == 14, turn(packed_dx, 11, 1), eastward)
     eastward = jnp.where(slot == 15, turn(packed_dy, 12, 1), eastward)
@@ -147,6 +205,20 @@
     to_east[0:8] = eastward
     to_east[8:16] = eastward_u
     to_west[...] = westward
+
+    @pl.when(announced > 0)
+    def _():
+        pl.semaphore_wait(barrier, announced)
+
+    @pl.when(leads_east)
+    def _():
+        send_east().start()
+
+    @pl.when(leads_west)
+    def _():
+        send_west().start()
+
+    loads[6].wait()
 
     for k in range(LEVELS):
         at = 8 * (k // 2) + 2 * (k % 2)
@@ -176,36 +248,13 @@
     def _():
         from_south[...] = jnp.zeros_like(from_south)
 
-    pl.semaphore_wait(barrier, jnp.where(bottom, 3, 4))
-
-    def remote(src, dst, index, device):
-        return pltpu.make_async_remote_copy(
-            src_ref=src, dst_ref=dst, send_sem=send_sem.at[index], recv_sem=recv_sem.at[index],
-            device_id=device, device_id_type=MESH,
-        )
-
-    send_east = remote(to_east, from_west, 0, east)
-    send_west = remote(to_west, from_east, 1, west)
-
-    send_north = remote(to_north, from_south, 2, (lon, jnp.minimum(lat + 1, lat_count - 1)))
-    send_south = remote(to_south, from_north, 3, (lon, jnp.maximum(lat - 1, 0)))
-    send_east.start()
-    send_west.start()
-
-    @pl.when(top)
-    def _():
-        pltpu.make_async_remote_copy(
-            src_ref=to_north.at[0:32], dst_ref=from_north, send_sem=send_sem.at[2], recv_sem=recv_sem.at[3],
-            device_id=mirror, device_id_type=MESH,
-        ).start()
-
-    @pl.when(jnp.logical_not(top))
-    def _():
-        send_north.start()
-
-    @pl.when(jnp.logical_not(bottom))
-    def _():
-        send_south.start()
+    @pl.when(leads_north)
+    def _():
+        start_northward()
+
+    @pl.when(leads_south)
+    def _():
+        send_south().start()
 
     def opened(x):
         return jnp.where(slot < 4, x, turn(x, 4, 1))
@@ -268,13 +317,13 @@
     lane_other = jnp.where(lane8 < 64, CONTRACTION, -EXPANSION)
 
     spans = ((2, 4, 29, 31), (1, 2, 0, 1), (2, 4, 30, 32), (0, 2, 0, 2), (2, 3, 31, 32), (0, 2, 1, 3))
-    places = (0, 1, 1, 2, 2, 3)
-    for place, (lo, hi, first, last) in zip(places, spans):
+    operand_ids = (0, 1, 1, 2, 2, 3)
+    for which, (lo, hi, first, last) in zip(operand_ids, spans):
         for tracer in range(2):
             at = 4 * tracer
             for k in range(LEVELS):
-                own_rows[place, k, at + lo : at + hi] = held[tracer, k, first:last]
-            own_geo[place, at + lo : at + hi] = depth[first:last]
+                own_rows[which, k, at + lo : at + hi] = held[tracer, k, first:last]
+            own_geo[which, at + lo : at + hi] = depth[first:last]
     for tracer in range(2):
         at = 4 * tracer
         for k in range(LEVELS):
@@ -292,9 +341,17 @@
 
     @pl.when(jnp.logical_not(bottom))
     def _():
-        remote(to_north, from_south, 2, (lon, lat)).wait_recv()
-
-    remote(to_south, from_north, 3, (lon, lat)).wait_recv()
+        send_north().wait_recv()
+
+    @pl.when(answers_south)
+    def _():
+        send_south().start()
+
+    send_south().wait_recv()
+
+    @pl.when(jnp.logical_not(leads_north))
+    def _():
+        start_northward()
 
     def spread(ref, index):
         return jnp.broadcast_to(ref[index : index + 1], (8, LANES))
@@ -349,8 +406,27 @@
             result[tracer, k, 0:2] += change[at : at + 2]
             result[tracer, k, ROWS - 2 : ROWS] += change[at + 2 : at + 4]
 
-    remote(to_east, from_west, 0, (lon, lat)).wait_recv()
-    remote(to_west, from_east, 1, (lon, lat)).wait_recv()
+    west_first = place == 3
+
+    @pl.when(west_first)
+    def _():
+        send_east().wait_recv()
+        send_west().start()
+
+    send_west().wait_recv()
+
+    @pl.when(answers_east)
+    def _():
+        send_east().start()
+
+    @pl.when(jnp.logical_not(west_first))
+    def _():
+        send_east().wait_recv()
+
+    @pl.when(place == 0)
+    def _():
+        send_west().start()
+
     came_w, came_u, came_e = from_west[0:8], from_west[8:16], from_east[...]
 
     def closed(own, low, high, low_from, high_from):
@@ -387,63 +463,70 @@
         change = flux - turn(flux, 1, 1)
         change = jnp.where(depth_x > float(k), weight_x * change, 0.0)
         change = jnp.where(slot < 4, change, turn(change, -4, 1))
-        for tracer in range(2):
+        changes[k] = change
+
+    send_east().wait_send()
+    send_west().wait_send()
+
+    @pl.when(top)
+    def _():
+        send_mirror().wait_send()
+
+    @pl.when(jnp.logical_not(top))
+    def _():
+        send_north().wait_send()
+
+    @pl.when(jnp.logical_not(bottom))
+    def _():
+        send_south().wait_send()
+
+
+def finish(result, changes, new_temp, new_salt):
+    lane = lax.broadcasted_iota(jnp.int32, (8, LANES), 1)
+    edge = (lane < 2) | (lane >= LANES - 2)
+    for k in range(LEVELS):
+        change = changes[k]
+        for tracer, new in enumerate((new_temp, new_salt)):
             for r in range(ROWS // 8):
                 moved = turn(change, 124 - 64 * tracer - 16 * r, 1)
-                result[tracer, k, 8 * r : 8 * r + 8] += jnp.where((lane8 < 2) | (lane8 >= 126), moved, 0.0)
-
-    stores = [
-        pltpu.make_async_copy(result.at[0], new_temp, out_sem.at[0]),
-        pltpu.make_async_copy(result.at[1], new_salt, out_sem.at[1]),
-    ]
-    for store in stores:
-        store.start()
-    send_east.wait_send()
-    send_west.wait_send()
-
-    @pl.when(top)
-    def _():
-        pltpu.make_async_remote_copy(
-            src_ref=to_north.at[0:32], dst_ref=from_north, send_sem=send_sem.at[2], recv_sem=recv_sem.at[3],
-            device_id=mirror, device_id_type=MESH,
-        ).wait_send()
-
-    @pl.when(jnp.logical_not(top))
-    def _():
-        send_north.wait_send()
-
-    @pl.when(jnp.logical_not(bottom))
-    def _():
-        send_south.wait_send()
-
-    for store in stores:
-        store.wait()
+                rows = slice(8 * r, 8 * r + 8)
+                new[k, rows] = result[tracer, k, rows] + jnp.where(edge, moved, 0.0)
 
 
 def local(temp, salt, east, north, dx, dy, depth):
     full = (LEVELS, ROWS, LANES)
     flat = (ROWS, LANES)
     shape = jax.ShapeDtypeStruct(full, F32)
-    scratch = [
-        pltpu.VMEM(full, F32), pltpu.VMEM(full, F32), pltpu.VMEM(full, F32), pltpu.VMEM(full, F32),
+    parts = ((2,) + full, (LEVELS, 8, LANES))
+    message = [pltpu.VMEM((rows, LANES), F32) for rows in (16, 8, 40, 32)]
+    scratch = [pltpu.VMEM(full, F32)] * 4 + [
         pltpu.VMEM(flat, F32), pltpu.VMEM(flat, F32), pltpu.VMEM(flat, jnp.int32),
-        pltpu.VMEM((2,) + full, F32), pltpu.VMEM((2,) + full, F32),
+        pltpu.VMEM((2,) + full, F32),
         pltpu.VMEM((LEVELS, 8, LANES), F32), pltpu.VMEM((LEVELS, 8, LANES), F32), pltpu.VMEM((3, 8, LANES), F32),
         pltpu.VMEM((4, LEVELS, 8, LANES), F32), pltpu.VMEM((LEVELS, 8, LANES), F32), pltpu.VMEM((10, 8, LANES), F32),
-        pltpu.VMEM((16, LANES), F32), pltpu.VMEM((8, LANES), F32), pltpu.VMEM((40, LANES), F32), pltpu.VMEM((32, LANES), F32),
-        pltpu.VMEM((16, LANES), F32), pltpu.VMEM((8, LANES), F32), pltpu.VMEM((40, LANES), F32), pltpu.VMEM((32, LANES), F32),
-        pltpu.SemaphoreType.DMA((7,)), pltpu.SemaphoreType.DMA((2,)),
-        pltpu.SemaphoreType.DMA((4,)), pltpu.SemaphoreType.DMA((4,)),
+        *message, *message,
+        pltpu.SemaphoreType.DMA((7,)), pltpu.SemaphoreType.DMA((4,)), pltpu.SemaphoreType.DMA((4,)),
     ]
+    inner = pl.BlockSpec(memory_space=pltpu.VMEM)
+    result, changes = pl.pallas_call(
+        kernel,
+        out_shape=tuple(pltpu.VMEM(part, F32) for part in parts),
+        in_specs=[pl.BlockSpec(memory_space=pltpu.HBM)] * 7,
+        out_specs=(inner, inner),
+        scratch_shapes=scratch,
+        compiler_params=pltpu.CompilerParams(
+            collective_id=0, has_side_effects=True, vmem_limit_bytes=16 * 2**20
+        ),
+        name="tracer_step",
+    )(*(pltpu.with_memory_space_constraint(x, pltpu.HBM) for x in (temp, salt, east, north, dx, dy, depth)))
     return pl.pallas_call(
-        kernel,
+        finish,
         out_shape=(shape, shape),
-        in_specs=[pl.BlockSpec(memory_space=pl.ANY)] * 7,
-        out_specs=(pl.BlockSpec(memory_space=pl.ANY),) * 2,
-        scratch_shapes=scratch,
-        compiler_params=pltpu.CompilerParams(collective_id=0, has_side_effects=True),
-        name="tracer_step",
-    )(temp, salt, east, north, dx, dy, depth)
+        in_specs=[inner, inner],
+        out_specs=(inner, inner),
+        compiler_params=pltpu.CompilerParams(vmem_limit_bytes=16 * 2**20),
+        name="edge_columns",
+    )(*(pltpu.with_memory_space_constraint(x, pltpu.VMEM) for x in (result, changes)))
 
 
 def solution(mesh):

time: 38.7 us -> 31.9 us (0.82)
  Pallas kernels: 35.7 us -> 31.1 us
  local copies, waits for them, and re-layouts: 2.22 us -> 0 us
    pallas_call x1 -> x2, Pallas kernels: 35.7 us -> 31.1 us  [the longest x1 30.3 us: local(): pl.pallas_call(kernel, out_shape=tuple((pltpu.VMEM(part, F32) for part in...]
    unnamed x4 -> x0, local copies, waits for them, and re-layouts: 2.22 us -> none
where the time goes in v2:
time: 31.9 us; the launch traced here: 31.7 us
  Pallas kernels  31.1 us (97%)
  between operations  0.64 us (2%)
    pallas_call x1, Pallas kernels, local(): pl.pallas_call(kernel, out_shape=tuple((pltpu.VMEM(part, F32) for part in...  30.3 us
    pallas_call x1, Pallas kernels, local(): pl.pallas_call(finish, out_shape=(shape, shape), in_specs=[inner, inner],...  0.79 us

profile of v2, /device:TPU:1, one launch (start us, length us, event | category | flops | bytes accessed | tf_op | source)
XLA Modules:
  0.0 31.7 jit_solution(10757815966744514100)
XLA Ops:
  0.6 30.3 %tracer_step.1 = (f32[2,6,32,128]{3,2,1,0:T(8,128)S(1)}, f32[6,8,128]{2,1,0:T(8,128)S(1)}) custom-call(f32[6,32,128]{2,1,0:T(8,128)} %temp_hbm.1, f32[6,32,128]{2,1,0:T(8,128)} %salt_hbm.1, f32[6,32,128]{2,1,0:T(8,128)} %east_hbm.1, f32[6,32,128]{2,1,0:T(8,128)} %north_hbm.1, f32[32,128]{1,0:T(8,128)} %dx_hbm.1, f32[32,128]{1,0:T(8,128)} %dy_hbm.1, ...), custom_call_target="tpu_custom_call" | custom-call | tf_op jit(solution)/shard_map/tracer_step/pallas_call | solution.py:511
  31.0 0.8 %edge_columns.1 = (f32[6,32,128]{2,1,0:T(8,128)}, f32[6,32,128]{2,1,0:T(8,128)}) custom-call(f32[2,6,32,128]{3,2,1,0:T(8,128)S(1)} %get-tuple-element.4.result, f32[6,8,128]{2,1,0:T(8,128)S(1)} %get-tuple-element.5.changes), custom_call_target="tpu_custom_call" | custom-call | tf_op jit(solution)/shard_map/edge_columns/pallas_call | solution.py:522

commit v3 on v2

--- a/solution.py
+++ b/solution.py
@@ -18,6 +18,7 @@
 LEVELS = 6
 ROWS = 32
 LANES = 128
+PIECE = 3
 
 
 def turn(x, shift, axis):
@@ -55,7 +56,7 @@
 
 def kernel(
     temp_hbm, salt_hbm, east_hbm, north_hbm, dx_hbm, dy_hbm, depth_hbm,
-    result, changes,
+    result,
     temp_in, salt_in, east_in, north_in, dx_in, dy_in, depth_in,
     held,
     pack_ts, pack_u, pack_g,
@@ -75,21 +76,25 @@
     bottom = lat == 0
 
     place = lax.rem(lon, 4)
-    even = lax.rem(lat, 2) == 0
+    early = place == 0
+    late = jnp.logical_not(early)
+    inner = jnp.logical_not(top)
+    raised = jnp.logical_not(bottom)
+    even = late & (lax.rem(lat, 2) == 0)
+    odd_row = late & (lax.rem(lat, 2) == 1)
     leads_east = place >= 2
     leads_west = (place == 1) | (place == 2)
-    leads_mirror = place >= 2
-    leads_north = even | (top & leads_mirror)
-    leads_south = even & jnp.logical_not(bottom)
-    answers_east = place <= 1
-    answers_west = (place == 0) | (place == 3)
-    answers_south = jnp.logical_not(even)
-
-    pairs = [
-        (depth_hbm, depth_in), (temp_hbm, temp_in), (salt_hbm, salt_in), (east_hbm, east_in),
-        (dx_hbm, dx_in), (dy_hbm, dy_in), (north_hbm, north_in),
-    ]
+    leads_mirror = top & (place >= 2)
+    answers_mirror = top & (place < 2)
+
+    pairs = [(depth_hbm, depth_in)]
+    for source, held_in in ((temp_hbm, temp_in), (salt_hbm, salt_in), (east_hbm, east_in)):
+        for first in range(0, LEVELS, PIECE):
+            part = pl.ds(first, PIECE)
+            pairs.append((source.at[part], held_in.at[part]))
+    pairs += [(dx_hbm, dx_in), (dy_hbm, dy_in)]
     loads = [pltpu.make_async_copy(a, b, in_sem.at[i]) for i, (a, b) in enumerate(pairs)]
+    late_load = pltpu.make_async_copy(north_hbm, north_in, in_sem.at[len(loads)])
     for load in loads:
         load.start()
 
@@ -98,32 +103,24 @@
     def greet(device):
         pl.semaphore_signal(barrier, inc=1, device_id=device, device_id_type=MESH)
 
-    @pl.when(answers_east)
-    def _():
-        greet(east)
-
-    @pl.when(answers_west)
-    def _():
-        greet(west)
-
-    @pl.when(jnp.logical_not(even))
-    def _():
-        greet(south)
-
-    @pl.when(jnp.logical_not(even | top))
-    def _():
-        greet(north)
-
-    @pl.when(top & jnp.logical_not(leads_mirror))
-    def _():
-        greet(mirror)
+    def greet_if(flag, device):
+        @pl.when(flag)
+        def _():
+            greet(device)
+
+    greet_if(place != 2, east)
+    greet_if(early | (place == 3), west)
+    greet_if(early & raised, (east[0], south[1]))
+    greet_if(early & inner, (east[0], north[1]))
+    greet_if(odd_row, south)
+    greet_if(odd_row & inner, north)
+    greet_if(answers_mirror, mirror)
 
     def one(flag):
         return jnp.where(flag, 1, 0)
 
-    announced = (
-        one(leads_east) + one(leads_west) + one(even) + one(leads_south) + one(top & leads_mirror)
-    )
+    announced = one(leads_east) + one(leads_west) + one(even) + one(even & raised) + one(leads_mirror)
+    announced = announced + one((place == 1) & raised) + one((place == 1) & inner)
 
     def remote(src, dst, out, into, device):
         return pltpu.make_async_remote_copy(
@@ -146,17 +143,14 @@
     def send_south():
         return remote(to_south, from_north, 3, 3, south)
 
-    def start_northward():
-        @pl.when(top)
+    def start_if(flag, send):
+        @pl.when(flag)
         def _():
-            send_mirror().start()
-
-        @pl.when(jnp.logical_not(top))
-        def _():
-            send_north().start()
-
-    for load in loads[:3]:
+            send().start()
+
+    for load in loads:
         load.wait()
+    late_load.start()
 
     lane8 = lax.broadcasted_iota(jnp.int32, (8, LANES), 1)
     sub8 = lax.broadcasted_iota(jnp.int32, (8, LANES), 0)
@@ -169,56 +163,45 @@
         held[0, k] = jnp.where(wet, temp_in[k], 0.0)
         held[1, k] = jnp.where(wet, salt_in[k], 0.0)
 
-    def gathered(blocks):
-        total = turn(blocks[0], 4, 1)
+    def gathered(blocks, base):
+        total = turn(blocks[0], base, 1)
         for g in range(1, len(blocks)):
-            total = jnp.where(group == g, turn(blocks[g], 16 * g + 4, 1), total)
+            total = jnp.where(group == g, turn(blocks[g], 16 * g + base, 1), total)
         return total
 
     def blocks_of(array):
         return [array[8 * r : 8 * r + 8] for r in range(ROWS // 8)]
 
-    packed = []
-    packed_u = []
-    for k in range(LEVELS):
-        packed.append(gathered(blocks_of(held[0, k]) + blocks_of(held[1, k])))
-    for load in loads[3:6]:
-        load.wait()
-    for k in range(LEVELS):
-        packed_u.append(gathered(blocks_of(east_in[k]) * 2))
     dx, dy = dx_in[...], dy_in[...]
-    packed_d = gathered(blocks_of(depth) * 2)
-    packed_dx = gathered(blocks_of(dx) * 2)
-    packed_dy = gathered(blocks_of(dy) * 2)
-
-    eastward, westward = turn(packed_d, 10, 1), turn(packed_d, 8, 1)
-    eastward = jnp.where(slot == 14, turn(packed_dx, 11, 1), eastward)
-    eastward = jnp.where(slot == 15, turn(packed_dy, 12, 1), eastward)
-    westward = jnp.where(slot == 14, turn(packed_dx, 10, 1), westward)
-    westward = jnp.where(slot == 15, turn(packed_dy, 11, 1), westward)
-    eastward_u = turn(packed_u[0], -3, 1)
-    for k in range(LEVELS):
-        eastward = jnp.where((slot >> 1) == k, turn(packed[k], 2 * k - 2, 1), eastward)
-        westward = jnp.where((slot >> 1) == k, turn(packed[k], 2 * k - 4, 1), westward)
-        if k:
-            eastward_u = jnp.where(slot == k, turn(packed_u[k], k - 3, 1), eastward_u)
-    to_east[0:8] = eastward
+    last, first = 1 - LANES, 0
+    blocks = [blocks_of(held[0, k]) + blocks_of(held[1, k]) for k in range(LEVELS)]
+    blocks_u = [blocks_of(east_in[k]) for k in range(LEVELS)]
+    blocks_d, blocks_dx, blocks_dy = blocks_of(depth) * 2, blocks_of(dx), blocks_of(dy)
+
+    def message(near, offset):
+        total = gathered(blocks_d, near + 12 + offset)
+        total = jnp.where(slot == 14, gathered(blocks_dx, near + 14), total)
+        total = jnp.where(slot == 15, gathered(blocks_dy, near + 15), total)
+        for k in range(LEVELS):
+            total = jnp.where((slot >> 1) == k, gathered(blocks[k], near + 2 * k + offset), total)
+        return total
+
+    eastward_u = gathered(blocks_u[0], last)
+    for k in range(1, LEVELS):
+        eastward_u = jnp.where(slot == k, gathered(blocks_u[k], last + k), eastward_u)
+    to_east[0:8] = message(last, 1)
     to_east[8:16] = eastward_u
-    to_west[...] = westward
-
-    @pl.when(announced > 0)
+
+    @pl.when(late)
     def _():
         pl.semaphore_wait(barrier, announced)
 
-    @pl.when(leads_east)
-    def _():
-        send_east().start()
-
-    @pl.when(leads_west)
-    def _():
-        send_west().start()
-
-    loads[6].wait()
+    start_if(leads_east, send_east)
+
+    to_west[...] = message(first, 0)
+    start_if(leads_west, send_west)
+
+    late_load.wait()
 
     for k in range(LEVELS):
         at = 8 * (k // 2) + 2 * (k % 2)
@@ -248,23 +231,30 @@
     def _():
         from_south[...] = jnp.zeros_like(from_south)
 
-    @pl.when(leads_north)
-    def _():
-        start_northward()
-
-    @pl.when(leads_south)
-    def _():
-        send_south().start()
-
-    def opened(x):
+    start_if(even, send_north)
+    start_if(even & raised, send_south)
+    start_if(leads_mirror, send_mirror)
+
+    def opened(blocks):
+        x = gathered(blocks, 4)
         return jnp.where(slot < 4, x, turn(x, 4, 1))
 
-    for k in range(LEVELS):
-        pack_ts[k] = opened(packed[k])
-        pack_u[k] = opened(packed_u[k])
-    pack_g[0] = opened(packed_d)
-    pack_g[1] = opened(packed_dx)
-    pack_g[2] = opened(packed_dy)
+    def doubled(x):
+        return jnp.where(lane8 < 64, x, turn(x, 64, 1))
+
+    def keep(ref, index, own):
+        ref[index] = own
+        ref[index + 1] = turn(own, -1, 1)
+
+    for k in range(LEVELS):
+        keep(pack_ts, 2 * k, opened(blocks[k]))
+        pack_u[k] = opened(blocks_u[k] * 2)
+    keep(pack_g, 0, opened(blocks_d))
+    keep(pack_g, 2, opened(blocks_dx * 2))
+    keep(pack_g, 4, opened(blocks_dy * 2))
+    own_depth, own_area = pack_g[0], pack_g[2] * pack_g[4]
+    pack_g[6] = jnp.where(slot < 4, own_depth, turn(own_depth, -4, 1))
+    pack_g[7] = -TIME_STEP / jnp.where(slot < 4, own_area, turn(own_area, -4, 1))
 
     lane = lax.broadcasted_iota(jnp.int32, (ROWS, LANES), 1)
     row = lax.broadcasted_iota(jnp.int32, (ROWS, LANES), 0)
@@ -339,19 +329,22 @@
         own_geo[9, at : at + 2] = depth[0:2]
         own_geo[9, at + 2 : at + 4] = depth[30:32]
 
-    @pl.when(jnp.logical_not(bottom))
+    @pl.when(early)
+    def _():
+        send_west().wait_recv()
+
+    start_if(early & inner, send_north)
+    start_if(early & raised, send_south)
+    start_if(early, send_east)
+
+    @pl.when(raised)
     def _():
         send_north().wait_recv()
 
-    @pl.when(answers_south)
-    def _():
-        send_south().start()
-
+    start_if(odd_row, send_south)
     send_south().wait_recv()
-
-    @pl.when(jnp.logical_not(leads_north))
-    def _():
-        start_northward()
+    start_if(odd_row & inner, send_north)
+    start_if(answers_mirror, send_mirror)
 
     def spread(ref, index):
         return jnp.broadcast_to(ref[index : index + 1], (8, LANES))
@@ -406,49 +399,53 @@
             result[tracer, k, 0:2] += change[at : at + 2]
             result[tracer, k, ROWS - 2 : ROWS] += change[at + 2 : at + 4]
 
-    west_first = place == 3
-
-    @pl.when(west_first)
+    @pl.when(early)
+    def _():
+        pl.semaphore_wait(barrier, 1)
+
+    start_if(early, send_west)
+
+    @pl.when(place == 3)
     def _():
         send_east().wait_recv()
-        send_west().start()
-
-    send_west().wait_recv()
-
-    @pl.when(answers_east)
-    def _():
-        send_east().start()
-
-    @pl.when(jnp.logical_not(west_first))
+
+    start_if(place == 3, send_west)
+
+    @pl.when(late)
+    def _():
+        send_west().wait_recv()
+
+    start_if(place == 1, send_east)
+
+    @pl.when(place != 3)
     def _():
         send_east().wait_recv()
 
-    @pl.when(place == 0)
-    def _():
-        send_west().start()
-
-    came_w, came_u, came_e = from_west[0:8], from_west[8:16], from_east[...]
-
-    def closed(own, low, high, low_from, high_from):
-        x = jnp.where((slot >> 1) == 3, turn(low, 6 - low_from, 1), own)
-        return jnp.where((slot >> 1) == 2, turn(high, 4 - high_from, 1), x)
-
-    depth_x = closed(pack_g[0], came_w, came_e, 12, 12)
-    own_dx, own_dy = pack_g[1], pack_g[2]
-    dx_x = closed(own_dx, came_w, came_e, 13, 14)
-    dy_x = closed(own_dy, came_w, came_e, 14, 15)
-    rlen = 2.0 / (dx_x + turn(dx_x, -1, 1))
-    breadth = 0.5 * (dy_x + turn(dy_x, -1, 1))
+    came_w, came_e = from_west[0:8], from_east[...]
+    came_u = doubled(from_west[8:16])
+    spread_w, spread_e = doubled(came_w), doubled(came_e)
+
+    def closed(pack, index, low, high, low_from, high_from):
+        here = jnp.where((slot >> 1) == 3, turn(low, 6 - low_from, 1), pack[index])
+        here = jnp.where((slot >> 1) == 2, turn(high, 4 - high_from, 1), here)
+        there = jnp.where(slot == 6, turn(low, 5 - low_from, 1), pack[index + 1])
+        there = jnp.where((slot == 3) | (slot == 4), turn(high, 3 - high_from, 1), there)
+        return here, there
+
+    depth_here, depth_there = closed(pack_g, 0, came_w, came_e, 12, 12)
+    dx_here, dx_there = closed(pack_g, 2, spread_w, spread_e, 13, 14)
+    dy_here, dy_there = closed(pack_g, 4, spread_w, spread_e, 14, 15)
+    rlen = 2.0 / (dx_here + dx_there)
     edge = (slot == 2) | (slot == 3) | (slot == 7) | (slot == 8)
-    breadth = jnp.where(edge, breadth, 0.0)
-    least = jnp.minimum(depth_x, turn(depth_x, -1, 1))
-    weight_x = -TIME_STEP / (dx_x * dy_x)
-    values = [closed(pack_ts[k], came_w, came_e, 2 * k, 2 * k) for k in range(LEVELS)]
-    nexts = [turn(x, -1, 1) for x in values]
-    gradients = vertical_quarter([x + y for x, y in zip(values, nexts)])
-    for k in range(LEVELS):
+    breadth = jnp.where(edge, 0.5 * (dy_here + dy_there), 0.0)
+    least = jnp.minimum(depth_here, depth_there)
+    cell_depth, cell_scale = pack_g[6], pack_g[7]
+    values = [closed(pack_ts, 2 * k, came_w, came_e, 2 * k, 2 * k) for k in range(LEVELS)]
+    gradients = vertical_quarter([x + y for x, y in values])
+    for k in range(LEVELS):
+        here, there = values[k]
         face = least > float(k)
-        jump = jnp.where(face, nexts[k] - values[k], 0.0)
+        jump = jnp.where(face, there - here, 0.0)
         gradient = gradients[k]
         speed = jnp.where(slot == 7, turn(came_u, 7 - k, 1), pack_u[k])
         upwind, factor = face_terms(speed, rlen)
@@ -457,62 +454,63 @@
             lane_mix * gradient + lane_other * turn(gradient, 64, 1),
         )
         flux = jnp.where(face, breadth, 0.0) * face_flux(
-            values[k], nexts[k], turn(jump, 1, 1), jump, turn(jump, -1, 1), gradient, slope, speed, upwind, factor,
-            rlen,
+            here, there, turn(jump, 1, 1), jump, turn(jump, -1, 1), gradient, slope, speed, upwind, factor, rlen
         )
-        change = flux - turn(flux, 1, 1)
-        change = jnp.where(depth_x > float(k), weight_x * change, 0.0)
-        change = jnp.where(slot < 4, change, turn(change, -4, 1))
-        changes[k] = change
-
-    send_east().wait_send()
-    send_west().wait_send()
-
-    @pl.when(top)
-    def _():
-        send_mirror().wait_send()
-
-    @pl.when(jnp.logical_not(top))
-    def _():
-        send_north().wait_send()
-
-    @pl.when(jnp.logical_not(bottom))
-    def _():
-        send_south().wait_send()
-
-
-def finish(result, changes, new_temp, new_salt):
-    lane = lax.broadcasted_iota(jnp.int32, (8, LANES), 1)
-    edge = (lane < 2) | (lane >= LANES - 2)
-    for k in range(LEVELS):
-        change = changes[k]
-        for tracer, new in enumerate((new_temp, new_salt)):
+        change = jnp.where(slot < 4, flux - turn(flux, 1, 1), turn(flux, -4, 1) - turn(flux, -3, 1))
+        change = jnp.where(cell_depth > float(k), cell_scale * change, 0.0)
+        for tracer in range(2):
             for r in range(ROWS // 8):
                 moved = turn(change, 124 - 64 * tracer - 16 * r, 1)
                 rows = slice(8 * r, 8 * r + 8)
-                new[k, rows] = result[tracer, k, rows] + jnp.where(edge, moved, 0.0)
+                result[tracer, k, rows] += jnp.where((lane8 < 2) | (lane8 >= LANES - 2), moved, 0.0)
+
+    send_east().wait_send()
+    send_west().wait_send()
+
+    @pl.when(top)
+    def _():
+        send_mirror().wait_send()
+
+    @pl.when(jnp.logical_not(top))
+    def _():
+        send_north().wait_send()
+
+    @pl.when(jnp.logical_not(bottom))
+    def _():
+        send_south().wait_send()
+
+
+def deliver(result, new_temp, new_salt, sem):
+    copies = []
+    for tracer, new in enumerate((new_temp, new_salt)):
+        for first in range(0, LEVELS, PIECE):
+            part = pl.ds(first, PIECE)
+            copies.append(pltpu.make_async_copy(result.at[tracer, part], new.at[part], sem.at[len(copies)]))
+    for copy in copies:
+        copy.start()
+    for copy in copies:
+        copy.wait()
 
 
 def local(temp, salt, east, north, dx, dy, depth):
     full = (LEVELS, ROWS, LANES)
     flat = (ROWS, LANES)
     shape = jax.ShapeDtypeStruct(full, F32)
-    parts = ((2,) + full, (LEVELS, 8, LANES))
     message = [pltpu.VMEM((rows, LANES), F32) for rows in (16, 8, 40, 32)]
     scratch = [pltpu.VMEM(full, F32)] * 4 + [
         pltpu.VMEM(flat, F32), pltpu.VMEM(flat, F32), pltpu.VMEM(flat, jnp.int32),
         pltpu.VMEM((2,) + full, F32),
-        pltpu.VMEM((LEVELS, 8, LANES), F32), pltpu.VMEM((LEVELS, 8, LANES), F32), pltpu.VMEM((3, 8, LANES), F32),
+        pltpu.VMEM((2 * LEVELS, 8, LANES), F32), pltpu.VMEM((LEVELS, 8, LANES), F32), pltpu.VMEM((8, 8, LANES), F32),
         pltpu.VMEM((4, LEVELS, 8, LANES), F32), pltpu.VMEM((LEVELS, 8, LANES), F32), pltpu.VMEM((10, 8, LANES), F32),
         *message, *message,
-        pltpu.SemaphoreType.DMA((7,)), pltpu.SemaphoreType.DMA((4,)), pltpu.SemaphoreType.DMA((4,)),
+        pltpu.SemaphoreType.DMA((3 * (LEVELS // PIECE) + 4,)), pltpu.SemaphoreType.DMA((4,)), pltpu.SemaphoreType.DMA((4,)),
     ]
     inner = pl.BlockSpec(memory_space=pltpu.VMEM)
-    result, changes = pl.pallas_call(
+    result = pl.pallas_call(
         kernel,
-        out_shape=tuple(pltpu.VMEM(part, F32) for part in parts),
+        out_shape=pltpu.VMEM((2,) + full, F32),
         in_specs=[pl.BlockSpec(memory_space=pltpu.HBM)] * 7,
-        out_specs=(inner, inner),
+        out_specs=inner,
         scratch_shapes=scratch,
         compiler_params=pltpu.CompilerParams(
             collective_id=0, has_side_effects=True, vmem_limit_bytes=16 * 2**20
@@ -520,13 +518,13 @@
         name="tracer_step",
     )(*(pltpu.with_memory_space_constraint(x, pltpu.HBM) for x in (temp, salt, east, north, dx, dy, depth)))
     return pl.pallas_call(
-        finish,
+        deliver,
         out_shape=(shape, shape),
-        in_specs=[inner, inner],
-        out_specs=(inner, inner),
-        compiler_params=pltpu.CompilerParams(vmem_limit_bytes=16 * 2**20),
-        name="edge_columns",
-    )(*(pltpu.with_memory_space_constraint(x, pltpu.VMEM) for x in (result, changes)))
+        in_specs=[inner],
+        out_specs=(pl.BlockSpec(memory_space=pltpu.HBM),) * 2,
+        scratch_shapes=[pltpu.SemaphoreType.DMA((2 * LEVELS // PIECE,))],
+        name="deliver",
+    )(pltpu.with_memory_space_constraint(result, pltpu.VMEM))
 
 
 def solution(mesh):

time: 31.9 us -> 31.4 us (0.984)
  Pallas kernels: 31.1 us -> 30.5 us
    pallas_call x2, Pallas kernels: 31.1 us -> 30.5 us  [the longest x1 29.8 us: local(): pl.pallas_call(kernel, out_shape=pltpu.VMEM((2,) + full, F32), in_specs=[...]
where the time goes in v3:
time: 31.4 us; the launch traced here: 31.2 us
  Pallas kernels  30.5 us (97%)
  between operations  0.64 us (2%)
    pallas_call x1, Pallas kernels, local(): pl.pallas_call(kernel, out_shape=pltpu.VMEM((2,) + full, F32), in_specs=[...  29.8 us
    pallas_call x1, Pallas kernels, local(): pl.pallas_call(deliver, out_shape=(shape, shape), in_specs=[inner], out_s...  0.71 us

profile of v3, /device:TPU:1, one launch (start us, length us, event | category | flops | bytes accessed | tf_op | source)
XLA Modules:
  0.0 31.2 jit_solution(1302450636509242604)
XLA Ops:
  0.6 29.8 %tracer_step.1.result = f32[2,6,32,128]{3,2,1,0:T(8,128)S(1)} custom-call(f32[6,32,128]{2,1,0:T(8,128)} %temp_hbm.1, f32[6,32,128]{2,1,0:T(8,128)} %salt_hbm.1, f32[6,32,128]{2,1,0:T(8,128)} %east_hbm.1, f32[6,32,128]{2,1,0:T(8,128)} %north_hbm.1, f32[32,128]{1,0:T(8,128)} %dx_hbm.1, f32[32,128]{1,0:T(8,128)} %dy_hbm.1, s32[32,128]{1,0:T(8,128)} %depth_hbm.1), custom_call_target="tpu_custom_call" | custom-call | tf_op jit(solution)/shard_map/tracer_step/pallas_call | solution.py:509
  30.5 0.7 %deliver.1 = (f32[6,32,128]{2,1,0:T(8,128)}, f32[6,32,128]{2,1,0:T(8,128)}) custom-call(f32[2,6,32,128]{3,2,1,0:T(8,128)S(1)} %tracer_step.1.result), custom_call_target="tpu_custom_call" | custom-call | tf_op jit(solution)/shard_map/deliver/pallas_call | solution.py:520

commit v4 on v3

--- a/solution.py
+++ b/solution.py
@@ -1,3 +1,5 @@
+import functools
+
 import jax
 import jax.numpy as jnp
 from jax import lax
@@ -54,9 +56,20 @@
     return [0.25 * (sums[min(k + 1, count - 1)] - sums[max(k - 1, 0)]) for k in range(count)]
 
 
+def fold_east(from_east, pack_ts, pack_g, slot, doubled):
+    came = from_east[...]
+    spread = doubled(came)
+    places = [(pack_ts, 2 * k, came, 2 * k) for k in range(LEVELS)]
+    places += [(pack_g, 0, came, 12), (pack_g, 2, spread, 14), (pack_g, 4, spread, 15)]
+    for pack, index, message, start in places:
+        pack[index] = jnp.where((slot >> 1) == 2, turn(message, 4 - start, 1), pack[index])
+        further = (slot == 3) | (slot == 4)
+        pack[index + 1] = jnp.where(further, turn(message, 3 - start, 1), pack[index + 1])
+
+
 def kernel(
     temp_hbm, salt_hbm, east_hbm, north_hbm, dx_hbm, dy_hbm, depth_hbm,
-    result,
+    result, changes,
     temp_in, salt_in, east_in, north_in, dx_in, dy_in, depth_in,
     held,
     pack_ts, pack_u, pack_g,
@@ -336,6 +349,8 @@
     start_if(early & inner, send_north)
     start_if(early & raised, send_south)
     start_if(early, send_east)
+    eastern_halo = functools.partial(fold_east, from_east, pack_ts, pack_g, slot, doubled)
+    pl.when(early)(eastern_halo)
 
     @pl.when(raised)
     def _():
@@ -421,26 +436,24 @@
     def _():
         send_east().wait_recv()
 
-    came_w, came_e = from_west[0:8], from_east[...]
+    pl.when(late)(eastern_halo)
+    came_w = from_west[0:8]
     came_u = doubled(from_west[8:16])
-    spread_w, spread_e = doubled(came_w), doubled(came_e)
-
-    def closed(pack, index, low, high, low_from, high_from):
-        here = jnp.where((slot >> 1) == 3, turn(low, 6 - low_from, 1), pack[index])
-        here = jnp.where((slot >> 1) == 2, turn(high, 4 - high_from, 1), here)
-        there = jnp.where(slot == 6, turn(low, 5 - low_from, 1), pack[index + 1])
-        there = jnp.where((slot == 3) | (slot == 4), turn(high, 3 - high_from, 1), there)
-        return here, there
-
-    depth_here, depth_there = closed(pack_g, 0, came_w, came_e, 12, 12)
-    dx_here, dx_there = closed(pack_g, 2, spread_w, spread_e, 13, 14)
-    dy_here, dy_there = closed(pack_g, 4, spread_w, spread_e, 14, 15)
+    spread_w = doubled(came_w)
+
+    def closed(pack, index, low, start):
+        here = jnp.where((slot >> 1) == 3, turn(low, 6 - start, 1), pack[index])
+        return here, jnp.where(slot == 6, turn(low, 5 - start, 1), pack[index + 1])
+
+    depth_here, depth_there = closed(pack_g, 0, came_w, 12)
+    dx_here, dx_there = closed(pack_g, 2, spread_w, 13)
+    dy_here, dy_there = closed(pack_g, 4, spread_w, 14)
     rlen = 2.0 / (dx_here + dx_there)
     edge = (slot == 2) | (slot == 3) | (slot == 7) | (slot == 8)
     breadth = jnp.where(edge, 0.5 * (dy_here + dy_there), 0.0)
     least = jnp.minimum(depth_here, depth_there)
     cell_depth, cell_scale = pack_g[6], pack_g[7]
-    values = [closed(pack_ts, 2 * k, came_w, came_e, 2 * k, 2 * k) for k in range(LEVELS)]
+    values = [closed(pack_ts, 2 * k, came_w, 2 * k) for k in range(LEVELS)]
     gradients = vertical_quarter([x + y for x, y in values])
     for k in range(LEVELS):
         here, there = values[k]
@@ -458,11 +471,7 @@
         )
         change = jnp.where(slot < 4, flux - turn(flux, 1, 1), turn(flux, -4, 1) - turn(flux, -3, 1))
         change = jnp.where(cell_depth > float(k), cell_scale * change, 0.0)
-        for tracer in range(2):
-            for r in range(ROWS // 8):
-                moved = turn(change, 124 - 64 * tracer - 16 * r, 1)
-                rows = slice(8 * r, 8 * r + 8)
-                result[tracer, k, rows] += jnp.where((lane8 < 2) | (lane8 >= LANES - 2), moved, 0.0)
+        changes[k] = change
 
     send_east().wait_send()
     send_west().wait_send()
@@ -480,14 +489,20 @@
         send_south().wait_send()
 
 
-def deliver(result, new_temp, new_salt, sem):
+def deliver(result, changes, new_temp, new_salt, patched, sem):
+    lane = lax.broadcasted_iota(jnp.int32, (8, LANES), 1)
+    edge = (lane < 2) | (lane >= LANES - 2)
     copies = []
-    for tracer, new in enumerate((new_temp, new_salt)):
-        for first in range(0, LEVELS, PIECE):
+    for first in range(0, LEVELS, PIECE):
+        for tracer, new in enumerate((new_temp, new_salt)):
+            for k in range(first, first + PIECE):
+                for r in range(ROWS // 8):
+                    moved = turn(changes[k], 124 - 64 * tracer - 16 * r, 1)
+                    rows = slice(8 * r, 8 * r + 8)
+                    patched[tracer, k, rows] = result[tracer, k, rows] + jnp.where(edge, moved, 0.0)
             part = pl.ds(first, PIECE)
-            copies.append(pltpu.make_async_copy(result.at[tracer, part], new.at[part], sem.at[len(copies)]))
-    for copy in copies:
-        copy.start()
+            copies.append(pltpu.make_async_copy(patched.at[tracer, part], new.at[part], sem.at[len(copies)]))
+            copies[-1].start()
     for copy in copies:
         copy.wait()
 
@@ -506,11 +521,11 @@
         pltpu.SemaphoreType.DMA((3 * (LEVELS // PIECE) + 4,)), pltpu.SemaphoreType.DMA((4,)), pltpu.SemaphoreType.DMA((4,)),
     ]
     inner = pl.BlockSpec(memory_space=pltpu.VMEM)
-    result = pl.pallas_call(
+    result, changes = pl.pallas_call(
         kernel,
-        out_shape=pltpu.VMEM((2,) + full, F32),
+        out_shape=(pltpu.VMEM((2,) + full, F32), pltpu.VMEM((LEVELS, 8, LANES), F32)),
         in_specs=[pl.BlockSpec(memory_space=pltpu.HBM)] * 7,
-        out_specs=inner,
+        out_specs=(inner, inner),
         scratch_shapes=scratch,
         compiler_params=pltpu.CompilerParams(
             collective_id=0, has_side_effects=True, vmem_limit_bytes=16 * 2**20
@@ -520,11 +535,11 @@
     return pl.pallas_call(
         deliver,
         out_shape=(shape, shape),
-        in_specs=[inner],
+        in_specs=[inner, inner],
         out_specs=(pl.BlockSpec(memory_space=pltpu.HBM),) * 2,
-        scratch_shapes=[pltpu.SemaphoreType.DMA((2 * LEVELS // PIECE,))],
+        scratch_shapes=[pltpu.VMEM((2,) + full, F32), pltpu.SemaphoreType.DMA((2 * LEVELS // PIECE,))],
         name="deliver",
-    )(pltpu.with_memory_space_constraint(result, pltpu.VMEM))
+    )(*(pltpu.with_memory_space_constraint(x, pltpu.VMEM) for x in (result, changes)))
 
 
 def solution(mesh):

time: 31.4 us -> 31.4 us (level)
  no operation moved by 1% of the time
where the time goes in v4:
time: 31.4 us; the launch traced here: 31.1 us
  Pallas kernels  30.5 us (97%)
  between operations  0.64 us (2%)
    pallas_call x1, Pallas kernels, local(): pl.pallas_call(kernel, out_shape=(pltpu.VMEM((2,) + full, F32), pltpu.VME...  29.7 us
    pallas_call x1, Pallas kernels, local(): pl.pallas_call(deliver, out_shape=(shape, shape), in_specs=[inner, inner]...  0.78 us

profile of v4, /device:TPU:1, one launch (start us, length us, event | category | flops | bytes accessed | tf_op | source)
XLA Modules:
  0.0 31.1 jit_solution(5942282441707873316)
XLA Ops:
  0.6 29.7 %tracer_step.1 = (f32[2,6,32,128]{3,2,1,0:T(8,128)S(1)}, f32[6,8,128]{2,1,0:T(8,128)S(1)}) custom-call(f32[6,32,128]{2,1,0:T(8,128)} %temp_hbm.1, f32[6,32,128]{2,1,0:T(8,128)} %salt_hbm.1, f32[6,32,128]{2,1,0:T(8,128)} %east_hbm.1, f32[6,32,128]{2,1,0:T(8,128)} %north_hbm.1, f32[32,128]{1,0:T(8,128)} %dx_hbm.1, f32[32,128]{1,0:T(8,128)} %dy_hbm.1, ...), custom_call_target="tpu_custom_call" | custom-call | tf_op jit(solution)/shard_map/tracer_step/pallas_call | solution.py:524
  30.3 0.8 %deliver.1 = (f32[6,32,128]{2,1,0:T(8,128)}, f32[6,32,128]{2,1,0:T(8,128)}) custom-call(f32[2,6,32,128]{3,2,1,0:T(8,128)S(1)} %get-tuple-element.4.result, f32[6,8,128]{2,1,0:T(8,128)S(1)} %get-tuple-element.5.changes), custom_call_target="tpu_custom_call" | custom-call | tf_op jit(solution)/shard_map/deliver/pallas_call | solution.py:535

commit v5 on v4

--- a/solution.py
+++ b/solution.py
@@ -71,7 +71,7 @@
     temp_hbm, salt_hbm, east_hbm, north_hbm, dx_hbm, dy_hbm, depth_hbm,
     result, changes,
     temp_in, salt_in, east_in, north_in, dx_in, dy_in, depth_in,
-    held,
+    held, west_in,
     pack_ts, pack_u, pack_g,
     own_rows, own_speed, own_geo,
     to_east, to_west, to_north, to_south,
@@ -414,64 +414,72 @@
             result[tracer, k, 0:2] += change[at : at + 2]
             result[tracer, k, ROWS - 2 : ROWS] += change[at + 2 : at + 4]
 
-    @pl.when(early)
-    def _():
-        pl.semaphore_wait(barrier, 1)
-
-    start_if(early, send_west)
-
-    @pl.when(place == 3)
-    def _():
-        send_east().wait_recv()
-
-    start_if(place == 3, send_west)
-
-    @pl.when(late)
-    def _():
-        send_west().wait_recv()
-
-    start_if(place == 1, send_east)
-
-    @pl.when(place != 3)
-    def _():
-        send_east().wait_recv()
-
-    pl.when(late)(eastern_halo)
-    came_w = from_west[0:8]
-    came_u = doubled(from_west[8:16])
-    spread_w = doubled(came_w)
-
-    def closed(pack, index, low, start):
-        here = jnp.where((slot >> 1) == 3, turn(low, 6 - start, 1), pack[index])
-        return here, jnp.where(slot == 6, turn(low, 5 - start, 1), pack[index + 1])
-
-    depth_here, depth_there = closed(pack_g, 0, came_w, 12)
-    dx_here, dx_there = closed(pack_g, 2, spread_w, 13)
-    dy_here, dy_there = closed(pack_g, 4, spread_w, 14)
-    rlen = 2.0 / (dx_here + dx_there)
-    edge = (slot == 2) | (slot == 3) | (slot == 7) | (slot == 8)
-    breadth = jnp.where(edge, 0.5 * (dy_here + dy_there), 0.0)
-    least = jnp.minimum(depth_here, depth_there)
-    cell_depth, cell_scale = pack_g[6], pack_g[7]
-    values = [closed(pack_ts, 2 * k, came_w, 2 * k) for k in range(LEVELS)]
-    gradients = vertical_quarter([x + y for x, y in values])
-    for k in range(LEVELS):
-        here, there = values[k]
-        face = least > float(k)
-        jump = jnp.where(face, there - here, 0.0)
-        gradient = gradients[k]
-        speed = jnp.where(slot == 7, turn(came_u, 7 - k, 1), pack_u[k])
-        upwind, factor = face_terms(speed, rlen)
-        slope = face_slope(
-            lane_mix * jump + lane_other * turn(jump, 64, 1), rlen,
-            lane_mix * gradient + lane_other * turn(gradient, 64, 1),
-        )
-        flux = jnp.where(face, breadth, 0.0) * face_flux(
-            here, there, turn(jump, 1, 1), jump, turn(jump, -1, 1), gradient, slope, speed, upwind, factor, rlen
-        )
-        change = jnp.where(slot < 4, flux - turn(flux, 1, 1), turn(flux, -4, 1) - turn(flux, -3, 1))
-        change = jnp.where(cell_depth > float(k), cell_scale * change, 0.0)
-        changes[k] = change
+    west_in[...] = to_east[...]
+
+    @pl.loop(0, 2)
+    def _(attempt):
+        @pl.when(attempt == 1)
+        def _():
+            @pl.when(early)
+            def _():
+                pl.semaphore_wait(barrier, 1)
+
+            start_if(early, send_west)
+
+            @pl.when(place == 3)
+            def _():
+                send_east().wait_recv()
+
+            start_if(place == 3, send_west)
+
+            @pl.when(late)
+            def _():
+                send_west().wait_recv()
+
+            start_if(place == 1, send_east)
+
+            @pl.when(place != 3)
+            def _():
+                send_east().wait_recv()
+
+            pl.when(late)(eastern_halo)
+            west_in[...] = from_west[...]
+
+        came_w = west_in[0:8]
+        came_u = doubled(west_in[8:16])
+        spread_w = doubled(came_w)
+
+        def closed(pack, index, low, start):
+            here = jnp.where((slot >> 1) == 3, turn(low, 6 - start, 1), pack[index])
+            return here, jnp.where(slot == 6, turn(low, 5 - start, 1), pack[index + 1])
+
+        depth_here, depth_there = closed(pack_g, 0, came_w, 12)
+        dx_here, dx_there = closed(pack_g, 2, spread_w, 13)
+        dy_here, dy_there = closed(pack_g, 4, spread_w, 14)
+        rlen = 2.0 / (dx_here + dx_there)
+        edge = (slot == 2) | (slot == 3) | (slot == 7) | (slot == 8)
+        breadth = jnp.where(edge, 0.5 * (dy_here + dy_there), 0.0)
+        least = jnp.minimum(depth_here, depth_there)
+        cell_depth, cell_scale = pack_g[6], pack_g[7]
+        values = [closed(pack_ts, 2 * k, came_w, 2 * k) for k in range(LEVELS)]
+        gradients = vertical_quarter([x + y for x, y in values])
+        for k in range(LEVELS):
+            here, there = values[k]
+            face = least > float(k)
+            jump = jnp.where(face, there - here, 0.0)
+            gradient = gradients[k]
+            speed = jnp.where(slot == 7, turn(came_u, 7 - k, 1), pack_u[k])
+            upwind, factor = face_terms(speed, rlen)
+            slope = face_slope(
+                lane_mix * jump + lane_other * turn(jump, 64, 1), rlen,
+                lane_mix * gradient + lane_other * turn(gradient, 64, 1),
+            )
+            flux = jnp.where(face, breadth, 0.0) * face_flux(
+                here, there, turn(jump, 1, 1), jump, turn(jump, -1, 1), gradient, slope, speed, upwind, factor, rlen
+            )
+            change = jnp.where(slot < 4, flux - turn(flux, 1, 1), turn(flux, -4, 1) - turn(flux, -3, 1))
+            change = jnp.where(cell_depth > float(k), cell_scale * change, 0.0)
+            changes[k] = change
 
     send_east().wait_send()
     send_west().wait_send()
@@ -514,7 +522,7 @@
     message = [pltpu.VMEM((rows, LANES), F32) for rows in (16, 8, 40, 32)]
     scratch = [pltpu.VMEM(full, F32)] * 4 + [
         pltpu.VMEM(flat, F32), pltpu.VMEM(flat, F32), pltpu.VMEM(flat, jnp.int32),
-        pltpu.VMEM((2,) + full, F32),
+        pltpu.VMEM((2,) + full, F32), pltpu.VMEM((16, LANES), F32),
         pltpu.VMEM((2 * LEVELS, 8, LANES), F32), pltpu.VMEM((LEVELS, 8, LANES), F32), pltpu.VMEM((8, 8, LANES), F32),
         pltpu.VMEM((4, LEVELS, 8, LANES), F32), pltpu.VMEM((LEVELS, 8, LANES), F32), pltpu.VMEM((10, 8, LANES), F32),
         *message, *message,

time: 31.4 us -> 31.4 us (level)
  no operation moved by 1% of the time
where the time goes in v5:
time: 31.4 us; the launch traced here: 31.1 us
  Pallas kernels  30.5 us (97%)
  between operations  0.64 us (2%)
    pallas_call x1, Pallas kernels, local(): pl.pallas_call(kernel, out_shape=(pltpu.VMEM((2,) + full, F32), pltpu.VME...  29.7 us
    pallas_call x1, Pallas kernels, local(): pl.pallas_call(deliver, out_shape=(shape, shape), in_specs=[inner, inner]...  0.78 us

profile of v5, /device:TPU:1, one launch (start us, length us, event | category | flops | bytes accessed | tf_op | source)
XLA Modules:
  0.0 31.1 jit_solution(12083191984072198359)
XLA Ops:
  0.6 29.7 %tracer_step.1 = (f32[2,6,32,128]{3,2,1,0:T(8,128)S(1)}, f32[6,8,128]{2,1,0:T(8,128)S(1)}) custom-call(f32[6,32,128]{2,1,0:T(8,128)} %temp_hbm.1, f32[6,32,128]{2,1,0:T(8,128)} %salt_hbm.1, f32[6,32,128]{2,1,0:T(8,128)} %east_hbm.1, f32[6,32,128]{2,1,0:T(8,128)} %north_hbm.1, f32[32,128]{1,0:T(8,128)} %dx_hbm.1, f32[32,128]{1,0:T(8,128)} %dy_hbm.1, ...), custom_call_target="tpu_custom_call" | custom-call | tf_op jit(solution)/shard_map/tracer_step/pallas_call | solution.py:532
  30.3 0.8 %deliver.1 = (f32[6,32,128]{2,1,0:T(8,128)}, f32[6,32,128]{2,1,0:T(8,128)}) custom-call(f32[2,6,32,128]{3,2,1,0:T(8,128)S(1)} %get-tuple-element.4.result, f32[6,8,128]{2,1,0:T(8,128)S(1)} %get-tuple-element.5.changes), custom_call_target="tpu_custom_call" | custom-call | tf_op jit(solution)/shard_map/deliver/pallas_call | solution.py:543

commit v6 on v5

--- a/solution.py
+++ b/solution.py
@@ -70,7 +70,7 @@
 def kernel(
     temp_hbm, salt_hbm, east_hbm, north_hbm, dx_hbm, dy_hbm, depth_hbm,
     result, changes,
-    temp_in, salt_in, east_in, north_in, dx_in, dy_in, depth_in,
+    fields, north_in, depth_in,
     held, west_in,
     pack_ts, pack_u, pack_g,
     own_rows, own_speed, own_geo,
@@ -100,14 +100,16 @@
     leads_mirror = top & (place >= 2)
     answers_mirror = top & (place < 2)
 
+    temp_in, salt_in, east_in = (fields.at[pl.ds(first, LEVELS)] for first in range(0, 3 * LEVELS, LEVELS))
+    dx_in, dy_in = fields.at[3 * LEVELS], fields.at[3 * LEVELS + 1]
     pairs = [(depth_hbm, depth_in)]
     for source, held_in in ((temp_hbm, temp_in), (salt_hbm, salt_in), (east_hbm, east_in)):
         for first in range(0, LEVELS, PIECE):
             part = pl.ds(first, PIECE)
             pairs.append((source.at[part], held_in.at[part]))
     pairs += [(dx_hbm, dx_in), (dy_hbm, dy_in)]
-    loads = [pltpu.make_async_copy(a, b, in_sem.at[i]) for i, (a, b) in enumerate(pairs)]
-    late_load = pltpu.make_async_copy(north_hbm, north_in, in_sem.at[len(loads)])
+    loads = [pltpu.make_async_copy(a, b, in_sem.at[min(i, 1)]) for i, (a, b) in enumerate(pairs)]
+    late_load = pltpu.make_async_copy(north_hbm, north_in, in_sem.at[2])
     for load in loads:
         load.start()
 
@@ -161,8 +163,8 @@
         def _():
             send().start()
 
-    for load in loads:
-        load.wait()
+    loads[0].wait()
+    pltpu.make_async_copy(fields, fields, in_sem.at[1]).wait()
     late_load.start()
 
     lane8 = lax.broadcasted_iota(jnp.int32, (8, LANES), 1)
@@ -520,13 +522,13 @@
     flat = (ROWS, LANES)
     shape = jax.ShapeDtypeStruct(full, F32)
     message = [pltpu.VMEM((rows, LANES), F32) for rows in (16, 8, 40, 32)]
-    scratch = [pltpu.VMEM(full, F32)] * 4 + [
-        pltpu.VMEM(flat, F32), pltpu.VMEM(flat, F32), pltpu.VMEM(flat, jnp.int32),
+    scratch = [
+        pltpu.VMEM((3 * LEVELS + 2,) + flat, F32), pltpu.VMEM(full, F32), pltpu.VMEM(flat, jnp.int32),
         pltpu.VMEM((2,) + full, F32), pltpu.VMEM((16, LANES), F32),
         pltpu.VMEM((2 * LEVELS, 8, LANES), F32), pltpu.VMEM((LEVELS, 8, LANES), F32), pltpu.VMEM((8, 8, LANES), F32),
         pltpu.VMEM((4, LEVELS, 8, LANES), F32), pltpu.VMEM((LEVELS, 8, LANES), F32), pltpu.VMEM((10, 8, LANES), F32),
         *message, *message,
-        pltpu.SemaphoreType.DMA((3 * (LEVELS // PIECE) + 4,)), pltpu.SemaphoreType.DMA((4,)), pltpu.SemaphoreType.DMA((4,)),
+        pltpu.SemaphoreType.DMA((3,)), pltpu.SemaphoreType.DMA((4,)), pltpu.SemaphoreType.DMA((4,)),
     ]
     inner = pl.BlockSpec(memory_space=pltpu.VMEM)
     result, changes = pl.pallas_call(

time: 31.4 us -> 31.3 us (level)
  no operation moved by 1% of the time
where the time goes in v6:
time: 31.3 us; the launch traced here: 31.1 us
  Pallas kernels  30.4 us (97%)
  between operations  0.64 us (2%)
    pallas_call x1, Pallas kernels, local(): pl.pallas_call(kernel, out_shape=(pltpu.VMEM((2,) + full, F32), pltpu.VME...  29.6 us
    pallas_call x1, Pallas kernels, local(): pl.pallas_call(deliver, out_shape=(shape, shape), in_specs=[inner, inner]...  0.78 us

profile of v6, /device:TPU:1, one launch (start us, length us, event | category | flops | bytes accessed | tf_op | source)
XLA Modules:
  0.0 31.1 jit_solution(7468163921093015385)
XLA Ops:
  0.6 29.6 %tracer_step.1 = (f32[2,6,32,128]{3,2,1,0:T(8,128)S(1)}, f32[6,8,128]{2,1,0:T(8,128)S(1)}) custom-call(f32[6,32,128]{2,1,0:T(8,128)} %temp_hbm.1, f32[6,32,128]{2,1,0:T(8,128)} %salt_hbm.1, f32[6,32,128]{2,1,0:T(8,128)} %east_hbm.1, f32[6,32,128]{2,1,0:T(8,128)} %north_hbm.1, f32[32,128]{1,0:T(8,128)} %dx_hbm.1, f32[32,128]{1,0:T(8,128)} %dy_hbm.1, ...), custom_call_target="tpu_custom_call" | custom-call | tf_op jit(solution)/shard_map/tracer_step/pallas_call | solution.py:534
  30.3 0.8 %deliver.1 = (f32[6,32,128]{2,1,0:T(8,128)}, f32[6,32,128]{2,1,0:T(8,128)}) custom-call(f32[2,6,32,128]{3,2,1,0:T(8,128)S(1)} %get-tuple-element.4.result, f32[6,8,128]{2,1,0:T(8,128)S(1)} %get-tuple-element.5.changes), custom_call_target="tpu_custom_call" | custom-call | tf_op jit(solution)/shard_map/deliver/pallas_call | solution.py:545
